TPU v7x, 128 devices: a whole 4x4x4 slice. The times are simulated.
128 devices in a mesh: dp: 8 (over y_hi, z), mp: 16 (over x, y_lo, core).
Axes of the slice: x: 4, y: 4 (y_hi: 2, y_lo: 2; y = y_hi * 2 + y_lo), z: 4, core: 2. Of those that a mesh axis runs over, the one named last changes fastest.
Arguments:
- z_a: float32 [1024, 16384], P('dp', 'mp'), may hold values from -60 to 60
- z_b: float32 [1024, 16384], P('dp', 'mp'), may hold values from -60 to 60
Outputs:
- dz_a: float32 [1024, 16384], P('dp', 'mp')
- dz_b: float32 [1024, 16384], P('dp', 'mp')
All inputs are finite; a program needn't handle non-finite values.
Results may differ from a plain program's by a relative error of at most 0.0054.
Values may be sent and summed in bfloat16 or wider, within the bound.
A program may use at most 192 MiB of HBM per device.

v0:
```python
import jax
import jax.numpy as jnp
from jax import lax
from jax.sharding import PartitionSpec as P

INVARIANCE_WEIGHT = 25.0
VARIANCE_WEIGHT = 25.0
DEVIATION_FLOOR = 0.0001
HUBER_EDGE = 0.05


def from_behind(block, axis, distance):
    devices = range(lax.axis_size(axis))
    route = [((i - distance) % len(devices), i) for i in devices]
    return lax.ppermute(block, axis, route)


def on_device(z_a, z_b):
    local_rows, feature_cols = z_a.shape
    dp_size = lax.axis_size("dp")
    model_parallel_count = lax.axis_size("mp")
    dp_index = lax.axis_index("dp")
    all_rows = local_rows * dp_size
    slab_width = feature_cols // dp_size
    slab_start = dp_index * slab_width
    stacked = jnp.stack([z_a, z_b], axis=1)
    col_sums = lax.psum(jnp.sum(stacked, axis=0), "dp")
    column_average = col_sums / all_rows
    centered = stacked - column_average[None]
    spread_squared = lax.psum(jnp.sum(centered * centered, axis=0), "dp") / (all_rows - 1)
    spread = jnp.sqrt(spread_squared + DEVIATION_FLOOR)
    var_term = (
        jnp.where(
            spread < 1.0, -(VARIANCE_WEIGHT * all_rows / (2.0 * (all_rows - 1))) / spread, 0.0
        )[None]
        * centered
    )
    centered_bf = centered.astype(jnp.bfloat16)
    gathered_samples = lax.all_gather(centered_bf, "dp", axis=0, tiled=True)
    own_slab = lax.dynamic_slice_in_dim(gathered_samples, slab_start, slab_width, 2)
    scaling = 2.0 * all_rows / (all_rows - 1.0)

    def coupling_factors(column_band, on_diagonal):
        gram_block = jnp.einsum(
            "tis,tio->iso", gathered_samples, column_band, preferred_element_type=jnp.float32
        )
        clipped = jnp.clip(gram_block / (all_rows - 1.0), -HUBER_EDGE, HUBER_EDGE)
        if on_diagonal:
            row_ids = jnp.arange(feature_cols, dtype=jnp.int32)[:, None]
            col_ids = slab_start + jnp.arange(slab_width, dtype=jnp.int32)[None, :]
            clipped = jnp.where((row_ids == col_ids)[None], 0.0, clipped)
        return (scaling * clipped).astype(jnp.bfloat16)

    diagonal_block_factor = coupling_factors(own_slab, True)
    portion_outcome = jnp.einsum(
        "esn,snr->esr", gathered_samples, diagonal_block_factor, preferred_element_type=jnp.float32
    )
    kept_slabs = []
    kept_weights = []
    half_turn = model_parallel_count // 2
    column_band = own_slab
    for offset in range(1, half_turn + 1):
        column_band = from_behind(own_slab, "mp", -offset)
        cross_factor = coupling_factors(column_band, False)
        toward = jnp.einsum(
            "esn,snr->esr", gathered_samples, cross_factor, preferred_element_type=jnp.float32
        )
        portion_outcome = portion_outcome + from_behind(toward, "mp", offset)
        if 2 * offset < model_parallel_count:
            kept_slabs.append(column_band)
            kept_weights.append(cross_factor)
    running = jnp.zeros((local_rows * lax.axis_size("dp"), 2, feature_cols), jnp.float32)
    for column_band, cross_factor in zip(kept_slabs, kept_weights):
        running = running + jnp.einsum(
            "yhi,hwi->yhw", column_band, cross_factor, preferred_element_type=jnp.float32
        )
    covariance_term = lax.psum_scatter(
        running.astype(jnp.bfloat16), "dp", scatter_dimension=0, tiled=True
    ).astype(jnp.float32)
    covariance_term = covariance_term + lax.all_to_all(
        portion_outcome, "dp", split_axis=0, concat_axis=2, tiled=True
    )
    gradient_sum = var_term + covariance_term
    difference = INVARIANCE_WEIGHT * (z_a - z_b)
    dz_a = difference + gradient_sum[:, 0]
    dz_b = gradient_sum[:, 1] - difference
    return (dz_a, dz_b)


def solution(mesh):
    in_specs = (P("dp", "mp"), P("dp", "mp"))
    out_specs = (P("dp", "mp"), P("dp", "mp"))
    return jax.shard_map(
        on_device, mesh=mesh, in_specs=in_specs, out_specs=out_specs, check_vma=False
    )
```

profile of v0, /device:TPU:25, one launch (start us, length us, event | category | flops | bytes accessed | tf_op | source)
XLA Modules:
  0.0 458.1 jit_solution(6024964497421023364)
XLA Ops:
  8.5 20.2 %psum.14 = f32[2,1024]{1,0:T(2,128)S(1)} all-reduce(f32[2,1024]{1,0:T(2,128)S(1)} %fusion.49), channel_id=1, replica_groups=mesh['dp'=8,'mp'=16] {'dp'}, use_global_device_ids=true, to_apply=%region_1.0 | all-reduce | flops 2048 | bytes 16384 | tf_op jit(solution)/shard_map/psum | solution.py:27
  30.9 71.9 %all-gather.2.cloned.1.call-done = bf16[1024,2,1024]{2,0,1:T(8,128)(2,1)} async-done(((bf16[128,2,1024]{2,0,1:T(8,128)(2,1)}), bf16[1024,2,1024]{2,0,1:T(8,128)(2,1)}) %all-gather.2.cloned.1.call-update) | async-done | bytes 4194320 | tf_op jit(solution)/shard_map/all_gather | solution.py:39
  109.5 4.7 %collective-permute-start.2 = (bf16[1024,2,128]{2,0,1:T(8,128)(2,1)S(1)}, bf16[1024,2,128]{2,0,1:T(8,128)(2,1)S(1)}, u32[]{:S(2)}, u32[]{:S(2)}) collective-permute-start(bf16[1024,2,128]{2,0,1:T(8,128)(2,1)S(1)} %constant_dynamic-slice_fusion), channel_id=1, source_target_pairs={{3,0},{4,1},{5,2},{6,3},{7,4},{8,5},{9,6},{10,7},{11,8},{12,9},{13... | collective-permute-start | bytes 1572872 | tf_op jit(solution)/shard_map/ppermute | solution.py:15
  114.2 9.1 %collective-permute-done.6 = bf16[1024,2,128]{2,0,1:T(8,128)(2,1)S(1)} collective-permute-done((bf16[1024,2,128]{2,0,1:T(8,128)(2,1)S(1)}, bf16[1024,2,128]{2,0,1:T(8,128)(2,1)S(1)}, u32[]{:S(2)}, u32[]{:S(2)}) %collective-permute-start.6) | collective-permute-done | bytes 524320 | tf_op jit(solution)/shard_map/ppermute | solution.py:15
  127.5 7.1 %collective-permute-done.5 = bf16[1024,2,128]{2,0,1:T(8,128)(2,1)S(1)} collective-permute-done((bf16[1024,2,128]{2,0,1:T(8,128)(2,1)S(1)}, bf16[1024,2,128]{2,0,1:T(8,128)(2,1)S(1)}, u32[]{:S(2)}, u32[]{:S(2)}) %collective-permute-start.5) | collective-permute-done | bytes 524320 | tf_op jit(solution)/shard_map/ppermute | solution.py:15
  136.9 9.0 %collective-permute-done.4 = bf16[1024,2,128]{2,0,1:T(8,128)(2,1)S(1)} collective-permute-done((bf16[1024,2,128]{2,0,1:T(8,128)(2,1)S(1)}, bf16[1024,2,128]{2,0,1:T(8,128)(2,1)S(1)}, u32[]{:S(2)}, u32[]{:S(2)}) %collective-permute-start.4) | collective-permute-done | bytes 524320 | tf_op jit(solution)/shard_map/ppermute | solution.py:15
  147.6 9.5 %collective-permute-done.3 = bf16[1024,2,128]{2,0,1:T(8,128)(2,1)S(1)} collective-permute-done((bf16[1024,2,128]{2,0,1:T(8,128)(2,1)S(1)}, bf16[1024,2,128]{2,0,1:T(8,128)(2,1)S(1)}, u32[]{:S(2)}, u32[]{:S(2)}) %collective-permute-start.3) | collective-permute-done | bytes 524320 | tf_op jit(solution)/shard_map/ppermute | solution.py:15
  160.6 16.8 %collective-permute-done.1 = bf16[1024,2,128]{2,0,1:T(8,128)(2,1)S(1)} collective-permute-done((bf16[1024,2,128]{2,0,1:T(8,128)(2,1)S(1)}, bf16[1024,2,128]{2,0,1:T(8,128)(2,1)S(1)}, u32[]{:S(2)}, u32[]{:S(2)}) %collective-permute-start.1) | collective-permute-done | bytes 524320 | tf_op jit(solution)/shard_map/ppermute | solution.py:15
  182.8 4.5 fusion.64
  187.3 4.7 %fusion.63 = f32[2,1024,1024]{1,2,0:T(8,128)} fusion(bf16[2,1024,128]{2,1,0:T(8,128)(2,1)S(1)} %fusion.32, bf16[1024,2,128]{2,0,1:T(8,128)(2,1)S(1)} %collective-permute-done.4), kind=kOutput, calls=%fused_computation.95 | convolution fusion | flops 536870912 | bytes 9437184 | tf_op jit(solution)/shard_map/yhi,hwi->yhw/dot_general | solution.py:74
  209.9 19.0 %fusion = bf16[1024,2,1024]{2,0,1:T(8,128)(2,1)} fusion(f32[2,1024,1024]{1,2,0:T(8,128)} %fusion.64, f32[2,1024,1024]{1,2,0:T(8,128)} %fusion.63, f32[2,1024,1024]{1,2,0:T(8,128)} %fusion.62, f32[2,1024,1024]{1,2,0:T(8,128)} %fusion.61, f32[2,1024,1024]{1,2,0:T(8,128)} %fusion.59, f32[2,1024,1024]{1,2,0:T(8,128)} %fusion.60, ...), kind=kOutput, calls=%fused_computation.1 | convolution fusion | flops 551550976 | bytes 55574528 | tf_op jit(solution)/shard_map/yhi,hwi->yhw/dot_general | solution.py:74
  230.8 4.7 %convolution_bitcast_fusion.1 = f32[1024,2,128]{0,2,1:T(8,128)} fusion(bf16[2,1024,128]{2,1,0:T(8,128)(2,1)S(1)} %fusion.34, bf16[1024,2,1024]{2,0,1:T(8,128)(2,1)} %all-gather.2.cloned.1.call-done), kind=kOutput, calls=%fused_computation.6 | convolution fusion | flops 536870912 | bytes 5767168 | tf_op jit(solution)/shard_map/esn,snr->esr/dot_general | solution.py:65
  259.1 7.6 %convolution_bitcast_fusion = f32[1024,2,128]{0,2,1:T(8,128)} fusion(bf16[1024,2,1024]{2,0,1:T(8,128)(2,1)} %all-gather.2.cloned.1.call-done, bf16[1024,2,128]{2,0,1:T(8,128)(2,1)} %copy-done.11), kind=kOutput, calls=%fused_computation.2 | convolution fusion | flops 1074790400 | bytes 5767168 | tf_op jit(solution)/shard_map/esn,snr->esr/dot_general | solution.py:65
  266.7 11.7 %collective-permute-done.13 = f32[1024,2,128]{0,2,1:T(8,128)} collective-permute-done((f32[1024,2,128]{0,2,1:T(8,128)}, f32[1024,2,128]{0,2,1:T(8,128)}, u32[]{:S(2)}, u32[]{:S(2)}) %collective-permute-start.13) | collective-permute-done | bytes 1048608 | tf_op jit(solution)/shard_map/ppermute | solution.py:15
  281.8 18.6 %collective-permute-start.7 = (f32[1024,2,128]{0,2,1:T(8,128)}, f32[1024,2,128]{0,2,1:T(8,128)S(1)}, u32[]{:S(2)}, u32[]{:S(2)}) collective-permute-start(f32[1024,2,128]{0,2,1:T(8,128)} %convolution_bitcast_fusion.7), channel_id=1, source_target_pairs={{15,0},{0,1},{1,2},{2,3},{3,4},{4,5},{5,6},{6,7},{7,8},{8,9},{9,10... | collective-permute-start | bytes 3145736 | tf_op jit(solution)/shard_map/ppermute | solution.py:15
  300.4 18.1 %collective-permute-done.11 = f32[1024,2,128]{0,2,1:T(8,128)} collective-permute-done((f32[1024,2,128]{0,2,1:T(8,128)}, f32[1024,2,128]{0,2,1:T(8,128)}, u32[]{:S(2)}, u32[]{:S(2)}) %collective-permute-start.11) | collective-permute-done | bytes 1048608 | tf_op jit(solution)/shard_map/ppermute | solution.py:15
  320.3 6.4 %collective-permute-done.10 = f32[1024,2,128]{0,2,1:T(8,128)} collective-permute-done((f32[1024,2,128]{0,2,1:T(8,128)}, f32[1024,2,128]{0,2,1:T(8,128)}, u32[]{:S(2)}, u32[]{:S(2)}) %collective-permute-start.10) | collective-permute-done | bytes 1048608 | tf_op jit(solution)/shard_map/ppermute | solution.py:15
  326.7 22.5 %collective-permute-done.9 = f32[1024,2,128]{0,2,1:T(8,128)S(1)} collective-permute-done((f32[1024,2,128]{0,2,1:T(8,128)}, f32[1024,2,128]{0,2,1:T(8,128)S(1)}, u32[]{:S(2)}, u32[]{:S(2)}) %collective-permute-start.9) | collective-permute-done | bytes 1048608 | tf_op jit(solution)/shard_map/ppermute | solution.py:15
  349.2 22.5 %collective-permute-done.8 = f32[1024,2,128]{0,2,1:T(8,128)S(1)} collective-permute-done((f32[1024,2,128]{0,2,1:T(8,128)}, f32[1024,2,128]{0,2,1:T(8,128)S(1)}, u32[]{:S(2)}, u32[]{:S(2)}) %collective-permute-start.8) | collective-permute-done | bytes 1048608 | tf_op jit(solution)/shard_map/ppermute | solution.py:15
  371.7 22.5 %collective-permute-done.7 = f32[1024,2,128]{0,2,1:T(8,128)S(1)} collective-permute-done((f32[1024,2,128]{0,2,1:T(8,128)}, f32[1024,2,128]{0,2,1:T(8,128)S(1)}, u32[]{:S(2)}, u32[]{:S(2)}) %collective-permute-start.7) | collective-permute-done | bytes 1048608 | tf_op jit(solution)/shard_map/ppermute | solution.py:15
  395.2 13.1 %collective-permute-done.15 = f32[1024,2,128]{0,2,1:T(8,128)} collective-permute-done((f32[1024,2,128]{0,2,1:T(8,128)}, f32[1024,2,128]{0,2,1:T(8,128)}, u32[]{:S(2)}, u32[]{:S(2)}) %collective-permute-start.15) | collective-permute-done | bytes 1048608 | tf_op jit(solution)/shard_map/ppermute | solution.py:15
  408.3 8.6 %fusion.27 = f32[1024,2,128]{0,2,1:T(8,128)S(1)} fusion(f32[1024,2,128]{0,2,1:T(8,128)} %collective-permute-done.15, f32[1024,2,128]{0,2,1:T(8,128)} %collective-permute-done.13, f32[1024,2,128]{0,2,1:T(8,128)} %collective-permute-done.12, f32[1024,2,128]{0,2,1:T(8,128)} %collective-permute-done.11, f32[1024,2,128]{0,2,1:T(8,128)} %collective-permute-done.10, ...), kind=kOutput, calls=%fused_computation.46 | convolution fusion | flops 1077149696 | bytes 14286848 | tf_op jit(solution)/shard_map/esn,snr->esr/dot_general | solution.py:55
  418.2 8.5 %all-to-all-start = ((f32[1024,2,128]{2,1,0:T(2,128)}), f32[1024,2,128]{2,1,0:T(2,128)S(1)}, u32[]{:S(2)}, u32[]{:S(2)}) async-start(f32[1024,2,128]{2,1,0:T(2,128)} %copy.51), calls=%async_computation.1 | async-start | bytes 2097152 | tf_op jit(solution)/shard_map/all_to_all | solution.py:80
  426.6 21.1 %psum.15 = f32[2,1024]{1,0:T(2,128)S(1)} all-reduce(f32[2,1024]{1,0:T(2,128)S(1)} %get-tuple-element.4), channel_id=1, replica_groups=mesh['dp'=8,'mp'=16] {'dp'}, use_global_device_ids=true, to_apply=%region_3.0 | all-reduce | flops 2048 | bytes 16384 | tf_op jit(solution)/shard_map/psum | solution.py:30
  (77 shorter events, 81.4 us)
Async XLA Ops:
  7.2 95.6 %all-gather.2.cloned.1.call-start = ((), (), s32[]{:S(2)}) async-start(), calls=%async_computation.2 | async-start | bytes 4718592 | tf_op jit(solution)/shard_map/all_gather | solution.py:39
  30.8 417.8 %reduce-scatter.2.cloned.1.call-start = ((), (), s32[]{:S(2)}) async-start(), calls=%async_computation.3 | async-start | bytes 4718592 | tf_op jit(solution)/shard_map/reduce_scatter | solution.py:77
  102.8 32.3 %copy-start = (bf16[1024,2,1024]{2,0,1:T(8,128)(2,1)S(1)}, bf16[1024,2,1024]{2,0,1:T(8,128)(2,1)}, u32[]{:S(2)}) copy-start(bf16[1024,2,1024]{2,0,1:T(8,128)(2,1)} %all-gather.2.cloned.1.call-done) | copy-start | bytes 12582916
  104.0 19.4 %collective-permute-start.6 = (bf16[1024,2,128]{2,0,1:T(8,128)(2,1)S(1)}, bf16[1024,2,128]{2,0,1:T(8,128)(2,1)S(1)}, u32[]{:S(2)}, u32[]{:S(2)}) collective-permute-start(bf16[1024,2,128]{2,0,1:T(8,128)(2,1)S(1)} %constant_dynamic-slice_fusion), channel_id=1, source_target_pairs={{7,0},{8,1},{9,2},{10,3},{11,4},{12,5},{13,6},{14,7},{15,8},{0,9},... | collective-permute-start | bytes 1572872 | tf_op jit(solution)/shard_map/ppermute | solution.py:15
  106.8 27.8 %collective-permute-start.5 = (bf16[1024,2,128]{2,0,1:T(8,128)(2,1)S(1)}, bf16[1024,2,128]{2,0,1:T(8,128)(2,1)S(1)}, u32[]{:S(2)}, u32[]{:S(2)}) collective-permute-start(bf16[1024,2,128]{2,0,1:T(8,128)(2,1)S(1)} %constant_dynamic-slice_fusion), channel_id=1, source_target_pairs={{6,0},{7,1},{8,2},{9,3},{10,4},{11,5},{12,6},{13,7},{14,8},{15,9},... | collective-permute-start | bytes 1572872 | tf_op jit(solution)/shard_map/ppermute | solution.py:15
  109.5 36.3 %collective-permute-start.4 = (bf16[1024,2,128]{2,0,1:T(8,128)(2,1)S(1)}, bf16[1024,2,128]{2,0,1:T(8,128)(2,1)S(1)}, u32[]{:S(2)}, u32[]{:S(2)}) collective-permute-start(bf16[1024,2,128]{2,0,1:T(8,128)(2,1)S(1)} %constant_dynamic-slice_fusion), channel_id=1, source_target_pairs={{5,0},{6,1},{7,2},{8,3},{9,4},{10,5},{11,6},{12,7},{13,8},{14,9},{... | collective-permute-start | bytes 1572872 | tf_op jit(solution)/shard_map/ppermute | solution.py:15
  109.5 47.6 %collective-permute-start.3 = (bf16[1024,2,128]{2,0,1:T(8,128)(2,1)S(1)}, bf16[1024,2,128]{2,0,1:T(8,128)(2,1)S(1)}, u32[]{:S(2)}, u32[]{:S(2)}) collective-permute-start(bf16[1024,2,128]{2,0,1:T(8,128)(2,1)S(1)} %constant_dynamic-slice_fusion), channel_id=1, source_target_pairs={{4,0},{5,1},{6,2},{7,3},{8,4},{9,5},{10,6},{11,7},{12,8},{13,9},{1... | collective-permute-start | bytes 1572872 | tf_op jit(solution)/shard_map/ppermute | solution.py:15
  109.5 49.3 %collective-permute-start.2 = (bf16[1024,2,128]{2,0,1:T(8,128)(2,1)S(1)}, bf16[1024,2,128]{2,0,1:T(8,128)(2,1)S(1)}, u32[]{:S(2)}, u32[]{:S(2)}) collective-permute-start(bf16[1024,2,128]{2,0,1:T(8,128)(2,1)S(1)} %constant_dynamic-slice_fusion), channel_id=1, source_target_pairs={{3,0},{4,1},{5,2},{6,3},{7,4},{8,5},{9,6},{10,7},{11,8},{12,9},{13... | collective-permute-start | bytes 1572872 | tf_op jit(solution)/shard_map/ppermute | solution.py:15
  123.4 54.0 %collective-permute-start.1 = (bf16[1024,2,128]{2,0,1:T(8,128)(2,1)S(1)}, bf16[1024,2,128]{2,0,1:T(8,128)(2,1)S(1)}, u32[]{:S(2)}, u32[]{:S(2)}) collective-permute-start(bf16[1024,2,128]{2,0,1:T(8,128)(2,1)S(1)} %constant_dynamic-slice_fusion), channel_id=1, source_target_pairs={{2,0},{3,1},{4,2},{5,3},{6,4},{7,5},{8,6},{9,7},{10,8},{11,9},{12,... | collective-permute-start | bytes 1572872 | tf_op jit(solution)/shard_map/ppermute | solution.py:15
  134.6 46.4 %collective-permute-start = (bf16[1024,2,128]{2,0,1:T(8,128)(2,1)S(1)}, bf16[1024,2,128]{2,0,1:T(8,128)(2,1)S(1)}, u32[]{:S(2)}, u32[]{:S(2)}) collective-permute-start(bf16[1024,2,128]{2,0,1:T(8,128)(2,1)S(1)} %constant_dynamic-slice_fusion), channel_id=1, source_target_pairs={{1,0},{2,1},{3,2},{4,3},{5,4},{6,5},{7,6},{8,7},{9,8},{10,9},{11,1... | collective-permute-start | bytes 1572872 | tf_op jit(solution)/shard_map/ppermute | solution.py:15
  136.8 45.9 %copy-start.4 = (bf16[2,1024,128]{2,1,0:T(8,128)(2,1)}, bf16[2,1024,128]{2,1,0:T(8,128)(2,1)S(1)}, u32[]{:S(2)}) copy-start(bf16[2,1024,128]{2,1,0:T(8,128)(2,1)S(1)} %fusion.33) | copy-start | bytes 1572868
  182.8 22.7 %copy-start.6 = (bf16[2,1024,128]{2,1,0:T(8,128)(2,1)}, bf16[2,1024,128]{2,1,0:T(8,128)(2,1)S(1)}, u32[]{:S(2)}) copy-start(bf16[2,1024,128]{2,1,0:T(8,128)(2,1)S(1)} %fusion.28) | copy-start | bytes 1572868
  229.0 29.0 %collective-permute-start.14 = (bf16[1024,2,128]{2,0,1:T(8,128)(2,1)S(1)}, bf16[1024,2,128]{2,0,1:T(8,128)(2,1)S(1)}, u32[]{:S(2)}, u32[]{:S(2)}) collective-permute-start(bf16[1024,2,128]{2,0,1:T(8,128)(2,1)S(1)} %constant_dynamic-slice_fusion), channel_id=1, source_target_pairs={{8,0},{9,1},{10,2},{11,3},{12,4},{13,5},{14,6},{15,7},{0,8},{1,9},... | collective-permute-start | bytes 1572872 | tf_op jit(solution)/shard_map/ppermute | solution.py:15
  235.5 42.8 %collective-permute-start.13 = (f32[1024,2,128]{0,2,1:T(8,128)}, f32[1024,2,128]{0,2,1:T(8,128)}, u32[]{:S(2)}, u32[]{:S(2)}) collective-permute-start(f32[1024,2,128]{0,2,1:T(8,128)} %convolution_bitcast_fusion.1), channel_id=1, source_target_pairs={{9,0},{10,1},{11,2},{12,3},{13,4},{14,5},{15,6},{0,7},{1,8},{2,9},... | collective-permute-start | bytes 3145736 | tf_op jit(solution)/shard_map/ppermute | solution.py:15
  238.1 43.7 %collective-permute-start.12 = (f32[1024,2,128]{0,2,1:T(8,128)}, f32[1024,2,128]{0,2,1:T(8,128)}, u32[]{:S(2)}, u32[]{:S(2)}) collective-permute-start(f32[1024,2,128]{0,2,1:T(8,128)} %convolution_bitcast_fusion.2), channel_id=1, source_target_pairs={{10,0},{11,1},{12,2},{13,3},{14,4},{15,5},{0,6},{1,7},{2,8},{3,9},... | collective-permute-start | bytes 3145736 | tf_op jit(solution)/shard_map/ppermute | solution.py:15
  243.5 75.0 %collective-permute-start.11 = (f32[1024,2,128]{0,2,1:T(8,128)}, f32[1024,2,128]{0,2,1:T(8,128)}, u32[]{:S(2)}, u32[]{:S(2)}) collective-permute-start(f32[1024,2,128]{0,2,1:T(8,128)} %convolution_bitcast_fusion.3), channel_id=1, source_target_pairs={{11,0},{12,1},{13,2},{14,3},{15,4},{0,5},{1,6},{2,7},{3,8},{4,9},{... | collective-permute-start | bytes 3145736 | tf_op jit(solution)/shard_map/ppermute | solution.py:15
  249.4 77.4 %collective-permute-start.10 = (f32[1024,2,128]{0,2,1:T(8,128)}, f32[1024,2,128]{0,2,1:T(8,128)}, u32[]{:S(2)}, u32[]{:S(2)}) collective-permute-start(f32[1024,2,128]{0,2,1:T(8,128)} %convolution_bitcast_fusion.4), channel_id=1, source_target_pairs={{12,0},{13,1},{14,2},{15,3},{0,4},{1,5},{2,6},{3,7},{4,8},{5,9},{6... | collective-permute-start | bytes 3145736 | tf_op jit(solution)/shard_map/ppermute | solution.py:15
  258.8 90.4 %collective-permute-start.9 = (f32[1024,2,128]{0,2,1:T(8,128)}, f32[1024,2,128]{0,2,1:T(8,128)S(1)}, u32[]{:S(2)}, u32[]{:S(2)}) collective-permute-start(f32[1024,2,128]{0,2,1:T(8,128)} %convolution_bitcast_fusion.5), channel_id=1, source_target_pairs={{13,0},{14,1},{15,2},{0,3},{1,4},{2,5},{3,6},{4,7},{5,8},{6,9},{7,... | collective-permute-start | bytes 3145736 | tf_op jit(solution)/shard_map/ppermute | solution.py:15
  278.4 93.4 %collective-permute-start.8 = (f32[1024,2,128]{0,2,1:T(8,128)}, f32[1024,2,128]{0,2,1:T(8,128)S(1)}, u32[]{:S(2)}, u32[]{:S(2)}) collective-permute-start(f32[1024,2,128]{0,2,1:T(8,128)} %convolution_bitcast_fusion.6), channel_id=1, source_target_pairs={{14,0},{15,1},{0,2},{1,3},{2,4},{3,5},{4,6},{5,7},{6,8},{7,9},{8,1... | collective-permute-start | bytes 3145736 | tf_op jit(solution)/shard_map/ppermute | solution.py:15
  281.8 112.4 %collective-permute-start.7 = (f32[1024,2,128]{0,2,1:T(8,128)}, f32[1024,2,128]{0,2,1:T(8,128)S(1)}, u32[]{:S(2)}, u32[]{:S(2)}) collective-permute-start(f32[1024,2,128]{0,2,1:T(8,128)} %convolution_bitcast_fusion.7), channel_id=1, source_target_pairs={{15,0},{0,1},{1,2},{2,3},{3,4},{4,5},{5,6},{6,7},{7,8},{8,9},{9,10... | collective-permute-start | bytes 3145736 | tf_op jit(solution)/shard_map/ppermute | solution.py:15
  318.5 89.8 %collective-permute-start.15 = (f32[1024,2,128]{0,2,1:T(8,128)}, f32[1024,2,128]{0,2,1:T(8,128)}, u32[]{:S(2)}, u32[]{:S(2)}) collective-permute-start(f32[1024,2,128]{0,2,1:T(8,128)} %convolution_bitcast_fusion), channel_id=1, source_target_pairs={{8,0},{9,1},{10,2},{11,3},{12,4},{13,5},{14,6},{15,7},{0,8},{1,9},... | collective-permute-start | bytes 3145736 | tf_op jit(solution)/shard_map/ppermute | solution.py:15
  416.8 31.7 %copy-start.2 = (f32[128,1024]{1,0:T(8,128)S(1)}, f32[128,1024]{1,0:T(8,128)}, u32[]{:S(2)}) copy-start(f32[128,1024]{1,0:T(8,128)} %param.3) | copy-start | bytes 1572868
  416.9 31.7 %copy-start.3 = (f32[128,1024]{1,0:T(8,128)S(1)}, f32[128,1024]{1,0:T(8,128)}, u32[]{:S(2)}) copy-start(f32[128,1024]{1,0:T(8,128)} %param.2) | copy-start | bytes 1572868
  418.2 29.6 %all-to-all-start = ((f32[1024,2,128]{2,1,0:T(2,128)}), f32[1024,2,128]{2,1,0:T(2,128)S(1)}, u32[]{:S(2)}, u32[]{:S(2)}) async-start(f32[1024,2,128]{2,1,0:T(2,128)} %copy.51), calls=%async_computation.1 | async-start | bytes 2097152 | tf_op jit(solution)/shard_map/all_to_all | solution.py:80
  (7 other events, 55.5 us)
Sparse Core Ops, SparseCore 0:
  30.9 71.7 all-gather.1
  229.1 169.0 reduce-scatter.1
where the time goes:
time: 462 us; the launch traced here: 458 us
  waiting for transfers between devices  246 us (53%)
  matrix products  96.9 us (21%)
  starting transfers between devices  48.8 us (11%)
  blocking collectives  41.2 us (9%)
  between operations  14.5 us (3%)
  other arithmetic  5.98 us (1%)
  local copies, waits for them, and re-layouts  5.12 us (1%)
    ppermute x16, waiting for transfers between devices, from_behind(): return lax.ppermute(block, axis, route)  174 us
    all_gather x1, waiting for transfers between devices, on_device(): gathered_samples = lax.all_gather(centered_bf, 'dp', axis=0, tiled=True)  71.9 us
    dot_general x7, matrix products, on_device(): jnp.einsum('yhi,hwi->yhw', column_band, cross_factor, preferred_element_t...  46.1 us
    ppermute x16, starting transfers between devices, from_behind(): return lax.ppermute(block, axis, route)  40.3 us
    dot_general x8, matrix products, on_device(): jnp.einsum('esn,snr->esr', gathered_samples, cross_factor, preferred_elem...  27.6 us
    psum x1, blocking collectives, on_device(): lax.psum(jnp.sum(centered * centered, axis=0), 'dp') / (all_rows - 1)  21.1 us
    psum x1, blocking collectives, on_device(): col_sums = lax.psum(jnp.sum(stacked, axis=0), 'dp')  20.2 us
    dot_general x7, matrix products, coupling_factors(): jnp.einsum('tis,tio->iso', gathered_samples, column_band, preferred_eleme...  14.5 us
  transfers between devices with their start and end apart: 19, of which 15 were waited for; matrix products, arithmetic and copies ran while one was open for 11% of the time, Pallas kernels for 0%

commit v1 on v0

v1 whole, which is shorter than its diff:
```python
import jax
import jax.numpy as jnp
from jax import lax
from jax.experimental import pallas as pl
from jax.experimental.pallas import tpu as pltpu
from jax.sharding import PartitionSpec as P

INVARIANCE_WEIGHT = 25.0
VARIANCE_WEIGHT = 25.0
DEVIATION_FLOOR = 0.0001
HUBER_EDGE = 0.05

MESH = pl.DeviceIdType.MESH
F32 = jnp.float32
BF16 = jnp.bfloat16
N_COPIES = 120


def kernel(za, zb, out_a, out_b, stats, zi, stage, jt, wt, part_out, part_in, own, rows_out, rows_in, ss, rs):
    dp = lax.axis_index("dp")
    mp = lax.axis_index("mp")
    yh, z = dp // 4, dp % 4
    x, yl, c = mp // 4, (mp // 2) % 2, mp % 2
    local_rows, cols = za.shape
    chunk = cols // 4
    n_rows = local_rows * 8

    def dev(yh_=None, z_=None, x_=None, yl_=None, c_=None):
        yh_ = yh if yh_ is None else yh_
        z_ = z if z_ is None else z_
        x_ = x if x_ is None else x_
        yl_ = yl if yl_ is None else yl_
        c_ = c if c_ is None else c_
        return (yh_ * 4 + z_, x_ * 4 + yl_ * 2 + c_)

    def plus(v, k):
        return (v + (k % 4)) % 4

    sent = []

    def copy(src, dst, device):
        i = len(sent)
        cp = pltpu.make_async_remote_copy(
            src_ref=src, dst_ref=dst, send_sem=ss.at[i], recv_sem=rs.at[i], device_id=device, device_id_type=MESH
        )
        cp.start()
        sent.append(cp)
        return cp

    zl, zr, xl, xr = plus(z, -1), plus(z, 1), plus(x, -1), plus(x, 1)
    oyh, oyl, oc = 1 - yh, 1 - yl, 1 - c
    dp_peers = [(a, b) for a in range(2) for b in range(4) if a or b]

    def peer(a, b):
        return oyh if a else yh, plus(z, b)

    partners = [dev(yh_=peer(a, b)[0], z_=peer(a, b)[1]) for a, b in dp_peers]
    partners += [dev(yl_=oyl), dev(yh_=oyh, yl_=oyl), dev(x_=xl), dev(x_=xr), dev(c_=oc)]
    barrier = pltpu.get_barrier_semaphore()
    for partner in partners:
        pl.semaphore_signal(barrier, inc=1, device_id=partner, device_id_type=MESH)

    for v, ref in enumerate((za, zb)):
        total = jnp.sum(ref[...], axis=0, keepdims=True)
        shifted = ref[...] - total * (1.0 / local_rows)
        stats[dp, v : v + 1, :] = total
        stats[dp, v + 2 : v + 3, :] = jnp.sum(shifted * shifted, axis=0, keepdims=True)
    pl.semaphore_wait(barrier, len(partners))
    cps = [copy(stats.at[dp], stats.at[dp], dev(yh_=peer(a, b)[0], z_=peer(a, b)[1])) for a, b in dp_peers]
    for cp in cps:
        cp.wait_recv()

    totals = jnp.zeros((2, cols), F32)
    for d in range(8):
        totals = totals + stats[d, 0:2, :]
    mean = totals * (1.0 / n_rows)
    squares = jnp.zeros((2, cols), F32)
    for d in range(8):
        gap = stats[d, 0:2, :] * (1.0 / local_rows) - mean
        squares = squares + (stats[d, 2:4, :] + local_rows * (gap * gap))
    spread = jnp.sqrt(squares / (n_rows - 1) + DEVIATION_FLOOR)
    pull = jnp.where(spread < 1.0, -(VARIANCE_WEIGHT * n_rows / (2.0 * (n_rows - 1))) / spread, 0.0)

    first = yh == 0
    for f in range(4):
        cut = slice(f * chunk, (f + 1) * chunk)
        ca = (za[:, cut] - mean[0:1, cut]).astype(BF16)
        cb = (zb[:, cut] - mean[1:2, cut]).astype(BF16)
        zi[f, c, yl, z, yh] = jnp.where(first, ca, cb)
        stage[f] = jnp.where(first, cb, ca)

    order = [plus(z, 1), plus(z, -1), plus(z, 2), z]
    y_copies = []
    for f in order:
        here = zi.at[f, c, yl, z, yh]
        y_copies.append(
            [
                copy(here, here, dev(yl_=oyl)),
                copy(stage.at[f], here, dev(yh_=oyh, yl_=oyl)),
                copy(stage.at[f], here, dev(yh_=oyh)),
            ]
        )

    def shard_send(f, to):
        a = copy(zi.at[f, c, yl, z], zi.at[f, c, yl, z], dev(z_=to))
        b = copy(zi.at[f, c, oyl, z], zi.at[f, c, oyl, z], dev(z_=to))
        return a, b

    shares = []

    def share(ref):
        shares.append(copy(ref, ref, dev(c_=oc)))

    right, left = {}, {}
    right_f = [plus(z, k) for k in (1, 2, 3, 0)]
    left_f = [plus(z, k) for k in (-1, 2, 0, 1)]

    from_left_f = [plus(z, k) for k in (0, 1, 2, 3)]
    from_right_f = [plus(z, k) for k in (0, 3, 1, 2)]

    def wait_y(j):
        for cp in y_copies[j]:
            cp.wait_recv()
        share(zi.at[order[j], c, :, z])

    wait_y(0)
    right[0] = shard_send(right_f[0], zr)
    wait_y(1)
    left[0] = shard_send(left_f[0], zl)
    wait_y(2)
    right[1] = shard_send(right_f[1], zr)
    left[1] = shard_send(left_f[1], zl)
    wait_y(3)

    half = chunk // 2
    j_copies = {}

    def slab_send(q):
        zq = plus(z, q)
        block = zi[z, c, yl, zq].reshape(2 * local_rows, chunk)
        jt[zq, x] = block.T
        j_copies[q] = [copy(jt.at[zq, x], jt.at[zq, x], dev(x_=xr)), copy(jt.at[zq, x], jt.at[zq, x], dev(x_=xl))]

    j_fwd = []

    def slab_forward(q):
        zq = plus(z, q)
        for cp in j_copies[q]:
            cp.wait_recv()
        lo, hi = pl.ds(0, half), pl.ds(half, half)
        j_fwd.append(copy(jt.at[zq, xl, lo], jt.at[zq, xl, lo], dev(x_=xr)))
        j_fwd.append(copy(jt.at[zq, xr, hi], jt.at[zq, xr, hi], dev(x_=xl)))

    slab_send(0)

    difference = INVARIANCE_WEIGHT * (za[...] - zb[...])
    out_a[...] = difference + pull[0:1, :] * (za[...] - mean[0:1, :])
    out_b[...] = pull[1:2, :] * (zb[...] - mean[1:2, :]) - difference

    def forward_right(f):
        ref = zi.at[f, c, yl, zl, 0]
        return copy(ref, ref, dev(z_=zr))

    def forward_left(f):
        ref = zi.at[f, c, yl, zr, 1]
        return copy(ref, ref, dev(z_=zl))

    fr, fl = {}, {}
    z2 = plus(z, 2)

    right[0][0].wait_recv()
    fr[3] = forward_right(from_left_f[0])
    slab_send(-1)
    left[0][0].wait_recv()
    fl[1] = forward_left(from_right_f[0])
    slab_send(1)
    slab_forward(0)
    right[0][1].wait_recv()
    share(zi.at[from_left_f[0], c, :, zl])
    left[0][1].wait_recv()
    share(zi.at[from_right_f[0], c, :, zr])

    right[1][0].wait_recv()
    fr[0] = forward_right(from_left_f[1])
    right[2] = shard_send(right_f[2], zr)
    left[1][0].wait_recv()
    fl[0] = forward_left(from_right_f[1])
    left[2] = shard_send(left_f[2], zl)
    right[1][1].wait_recv()
    share(zi.at[from_left_f[1], c, :, zl])
    left[1][1].wait_recv()
    share(zi.at[from_right_f[1], c, :, zr])
    slab_forward(-1)
    slab_forward(1)

    across = {}

    def opposite(q):
        fr[q].wait_recv()
        fl[q].wait_recv()
        ref = zi.at[plus(z, q), c, yl, z2]
        across[q] = copy(ref, ref, dev(yl_=oyl))
        share(ref)

    def across_done(q):
        across[q].wait_recv()
        share(zi.at[plus(z, q), c, oyl, z2])

    opposite(0)
    slab_send(2)
    right[3] = shard_send(right_f[3], zr)
    left[3] = shard_send(left_f[3], zl)
    across_done(0)

    right[2][0].wait_recv()
    fr[1] = forward_right(from_left_f[2])
    left[2][0].wait_recv()
    fl[2] = forward_left(from_right_f[2])
    slab_forward(2)
    right[2][1].wait_recv()
    share(zi.at[from_left_f[2], c, :, zl])
    left[2][1].wait_recv()
    share(zi.at[from_right_f[2], c, :, zr])

    scale = 2.0 * n_rows / (n_rows - 1.0)
    slope = scale / (n_rows - 1.0)
    edge = HUBER_EDGE * scale

    def gram(f, cc, yy, first_part, parts):
        size = parts * chunk
        g = jnp.zeros((size, chunk), F32)
        for q in range(4):
            lhs = jt[q, pl.ds(first_part, parts)].reshape(size, chunk)
            rhs = zi[f, cc, yy, q].reshape(2 * local_rows, chunk)
            g = g + jnp.dot(lhs, rhs, preferred_element_type=F32)
        w = jnp.clip(g * slope, -edge, edge).astype(BF16)
        wt[f, cc, yy, pl.ds(first_part, parts)] = w.reshape(parts, chunk, chunk)

    def gram_blocks(f, yy):
        def body(i, carry):
            gram(f, i // 2, yy, (i % 2) * 2, 2)
            return carry

        lax.fori_loop(0, 4, body, 0)

    def gram_part(f, yy, part):
        def body(cc, carry):
            gram(f, cc, yy, part, 1)
            return carry

        lax.fori_loop(0, 2, body, 0)

    opposite(1)
    across_done(1)

    shared = iter(shares)

    n_seen = [0]

    def sibling(n):
        while n_seen[0] < n:
            next(shared).wait_recv()
            n_seen[0] += 1

    for cp in j_fwd:
        cp.wait_recv()
    sibling(10)
    gram_blocks(z, yl)
    gram_blocks(z, oyl)
    row_id = lax.broadcasted_iota(jnp.int32, (chunk, chunk), 0)
    col_id = lax.broadcasted_iota(jnp.int32, (chunk, chunk), 1)
    wt[z, c, yl, x] = jnp.where(row_id == col_id, jnp.zeros((), BF16), wt[z, c, yl, x])

    right[3][0].wait_recv()
    fr[2] = forward_right(from_left_f[3])
    left[3][0].wait_recv()
    fl[3] = forward_left(from_right_f[3])
    sibling(14)
    gram_blocks(plus(z, 1), yl)
    gram_blocks(plus(z, 1), oyl)
    right[3][1].wait_recv()
    share(zi.at[from_left_f[3], c, :, zl])
    left[3][1].wait_recv()
    share(zi.at[from_right_f[3], c, :, zr])
    opposite(2)
    opposite(3)
    sibling(18)
    gram_blocks(plus(z, 2), yl)
    gram_blocks(plus(z, 3), yl)
    across_done(2)
    across_done(3)
    sibling(20)
    x2 = plus(x, 2)
    gram_part(plus(z, 2), oyl, x2)
    gram_part(plus(z, 3), oyl, x2)

    def product(part, h):
        acc = jnp.zeros((4 * local_rows, chunk), F32)
        for f in range(4):
            for cc in range(2):
                for yy in range(2):
                    lhs = zi[f, cc, yy, 2 * h : 2 * h + 2].reshape(4 * local_rows, chunk)
                    acc = acc + lax.dot_general(
                        lhs, wt[f, cc, yy, part], (((1,), (1,)), ((), ())), preferred_element_type=F32
                    )
        return acc

    def send_part(slot, to, land):
        return copy(part_out.at[slot], part_in.at[land], dev(x_=to))

    part_out[0] = product(x2, 0).astype(BF16)
    r0 = send_part(0, xr, 0)
    part_out[1] = product(x2, 1).astype(BF16)
    l0 = send_part(1, xl, 3)
    for part in (xr, xl, x):
        gram_part(plus(z, 2), oyl, part)
        gram_part(plus(z, 3), oyl, part)
    part_out[2] = product(xr, 1).astype(BF16)
    r1 = send_part(2, xr, 1)
    part_out[3] = product(xl, 0).astype(BF16)
    l1 = send_part(3, xl, 4)
    acc = product(xr, 0)
    r0.wait_recv()
    part_out[4] = (acc + part_in[0].astype(F32)).astype(BF16)
    r2 = send_part(4, xr, 2)
    acc = product(xl, 1)
    l0.wait_recv()
    part_out[5] = (acc + part_in[3].astype(F32)).astype(BF16)
    l2 = send_part(5, xl, 5)
    own[0] = product(x, 0)
    own[1] = product(x, 1)
    r1.wait_recv()
    l1.wait_recv()
    own[0] = own[0] + part_in[4].astype(F32)
    own[1] = own[1] + part_in[1].astype(F32)
    r2.wait_recv()
    rows_out[0:2] = (own[0] + part_in[2].astype(F32)).astype(BF16).reshape(2, 2, local_rows, chunk)
    l2.wait_recv()
    rows_out[2:4] = (own[1] + part_in[5].astype(F32)).astype(BF16).reshape(2, 2, local_rows, chunk)

    back = []
    for a, b in dp_peers:
        pyh, pz = peer(a, b)
        back.append(copy(rows_out.at[pz, pyh], rows_in.at[yh, z], dev(yh_=pyh, z_=pz)))
    rows_in[yh, z] = rows_out[z, yh]
    for cp in back:
        cp.wait_recv()
    for f in range(4):
        cut = slice(f * chunk, (f + 1) * chunk)
        out_a[:, cut] = out_a[:, cut] + rows_in[0, f].astype(F32)
        out_b[:, cut] = out_b[:, cut] + rows_in[1, f].astype(F32)
    for cp in sent:
        cp.wait_send()


def on_device(z_a, z_b):
    rows, cols = z_a.shape
    chunk = cols // 4
    vmem = pl.BlockSpec(memory_space=pltpu.VMEM)
    return pl.pallas_call(
        kernel,
        out_shape=[jax.ShapeDtypeStruct((rows, cols), F32)] * 2,
        in_specs=[vmem, vmem],
        out_specs=[vmem, vmem],
        scratch_shapes=[
            pltpu.VMEM((8, 4, cols), F32),
            pltpu.VMEM((4, 2, 2, 4, 2, rows, chunk), BF16),
            pltpu.VMEM((4, rows, chunk), BF16),
            pltpu.VMEM((4, 4, chunk, 2 * rows), BF16),
            pltpu.VMEM((4, 2, 2, 4, chunk, chunk), BF16),
            pltpu.VMEM((6, 4 * rows, chunk), BF16),
            pltpu.VMEM((6, 4 * rows, chunk), BF16),
            pltpu.VMEM((2, 4 * rows, chunk), F32),
            pltpu.VMEM((4, 2, rows, chunk), BF16),
            pltpu.VMEM((2, 4, rows, chunk), BF16),
            pltpu.SemaphoreType.DMA((N_COPIES,)),
            pltpu.SemaphoreType.DMA((N_COPIES,)),
        ],
        compiler_params=pltpu.CompilerParams(collective_id=0, has_side_effects=True, vmem_limit_bytes=56 * 1024 * 1024),
        name="vicreg",
    )(z_a, z_b)


def solution(mesh):
    specs = (P("dp", "mp"), P("dp", "mp"))
    return jax.shard_map(on_device, mesh=mesh, in_specs=specs, out_specs=specs, check_vma=False)
```

time: 462 us -> 107 us (0.23)
  the two profiles are of different devices: /device:TPU:25 before, /device:TPU:0 now
where the time goes in v1:
time: 107 us; the launch traced here: 106 us
  Pallas kernels  103 us (96%)
  local copies, waits for them, and re-layouts  2.74 us (3%)
    pallas_call x1, Pallas kernels, on_device(): pl.pallas_call(kernel, out_shape=[jax.ShapeDtypeStruct((rows, cols), F32)...  103 us
    unnamed x4, local copies, waits for them, and re-layouts  2.74 us

profile of v1, /device:TPU:0, one launch (start us, length us, event | category | flops | bytes accessed | tf_op | source)
XLA Modules:
  0.0 106.2 jit_solution(14440166618219775071)
XLA Ops:
  0.6 102.9 %vicreg.1 = (f32[128,1024]{1,0:T(8,128)}, f32[128,1024]{1,0:T(8,128)}) custom-call(f32[128,1024]{1,0:T(8,128)} %za.1, f32[128,1024]{1,0:T(8,128)} %zb.1), custom_call_target="tpu_custom_call" | custom-call | tf_op jit(solution)/shard_map/vicreg/pallas_call | solution.py:360
  103.5 0.0 copy-start
  103.5 1.9 %copy.6 = f32[128,1024]{1,0:T(8,128)} copy(f32[128,1024]{1,0:T(8,128)} %get-tuple-element.4) | data formatting | bytes 1048576
  105.4 0.0 copy-done
  105.4 0.8 copy.7
Async XLA Ops:
  103.5 2.0 %copy-start = (f32[128,1024]{1,0:T(8,128)S(1)}, f32[128,1024]{1,0:T(8,128)}, u32[]{:S(2)}) copy-start(f32[128,1024]{1,0:T(8,128)} %get-tuple-element.5) | copy-start | bytes 1572868

commit v2 on v1

v2 whole, which is shorter than its diff:
```python
import jax
import jax.numpy as jnp
from jax import lax
from jax.experimental import pallas as pl
from jax.experimental.pallas import tpu as pltpu
from jax.sharding import PartitionSpec as P

INVARIANCE_WEIGHT = 25.0
VARIANCE_WEIGHT = 25.0
DEVIATION_FLOOR = 0.0001
HUBER_EDGE = 0.05

MESH = pl.DeviceIdType.MESH
F32 = jnp.float32
BF16 = jnp.bfloat16
N_COPIES = 128


def kernel(za_hbm, zb_hbm, cov, coefs, za, zb, stats, zi, stage, jt, wt, part_out, part_in, rows_out, rows_in, ls, ss, rs):
    dp = lax.axis_index("dp")
    mp = lax.axis_index("mp")
    yh, z = dp // 4, dp % 4
    x, yl, c = mp // 4, (mp // 2) % 2, mp % 2
    local_rows, cols = za.shape
    chunk = cols // 4
    n_rows = local_rows * 8
    pair = 2 * local_rows

    def dev(yh_=None, z_=None, x_=None, yl_=None, c_=None):
        yh_ = yh if yh_ is None else yh_
        z_ = z if z_ is None else z_
        x_ = x if x_ is None else x_
        yl_ = yl if yl_ is None else yl_
        c_ = c if c_ is None else c_
        return (yh_ * 4 + z_, x_ * 4 + yl_ * 2 + c_)

    def plus(v, k):
        return (v + (k % 4)) % 4

    sent = []

    def copy(src, dst, device):
        i = len(sent)
        cp = pltpu.make_async_remote_copy(
            src_ref=src, dst_ref=dst, send_sem=ss.at[i], recv_sem=rs.at[i], device_id=device, device_id_type=MESH
        )
        cp.start()
        sent.append(cp)
        return cp

    zl, zr, z2 = plus(z, -1), plus(z, 1), plus(z, 2)
    xl, xr, x2 = plus(x, -1), plus(x, 1), plus(x, 2)
    oyh, oyl, oc = 1 - yh, 1 - yl, 1 - c
    dp_peers = [(a, b) for a in range(2) for b in range(4) if a or b]

    def peer(a, b):
        return oyh if a else yh, plus(z, b)

    partners = [dev(yh_=peer(a, b)[0], z_=peer(a, b)[1]) for a, b in dp_peers]
    partners += [dev(yl_=oyl), dev(yh_=oyh, yl_=oyl), dev(x_=xl), dev(x_=xr), dev(c_=oc)]
    barrier = pltpu.get_barrier_semaphore()
    for partner in partners:
        pl.semaphore_signal(barrier, inc=1, device_id=partner, device_id_type=MESH)

    loads = [pltpu.make_async_copy(za_hbm, za, ls.at[0]), pltpu.make_async_copy(zb_hbm, zb, ls.at[1])]
    for load in loads:
        load.start()

    for v, ref in enumerate((za, zb)):
        loads[v].wait()
        total = jnp.sum(ref[...], axis=0, keepdims=True)
        shifted = ref[...] - total * (1.0 / local_rows)
        stats[dp, v : v + 1, :] = total
        stats[dp, v + 2 : v + 3, :] = jnp.sum(shifted * shifted, axis=0, keepdims=True)
    pl.semaphore_wait(barrier, len(partners))
    cps = [copy(stats.at[dp], stats.at[dp], dev(yh_=peer(a, b)[0], z_=peer(a, b)[1])) for a, b in dp_peers]
    for cp in cps:
        cp.wait_recv()

    totals = jnp.zeros((2, cols), F32)
    for d in range(8):
        totals = totals + stats[d, 0:2, :]
    mean = totals * (1.0 / n_rows)

    first = yh == 0
    for f in range(4):
        cut = slice(f * chunk, (f + 1) * chunk)
        ca = (za[:, cut] - mean[0:1, cut]).astype(BF16)
        cb = (zb[:, cut] - mean[1:2, cut]).astype(BF16)
        zi[f, c, yl, z, yh] = jnp.where(first, ca, cb)
        stage[f] = jnp.where(first, cb, ca)

    right_f = [plus(z, k) for k in (1, 2, 3, 0)]
    left_f = [plus(z, k) for k in (-1, 2, 0, 1)]
    from_left_f = [plus(z, k) for k in (0, 1, 2, 3)]
    from_right_f = [plus(z, k) for k in (0, 3, 1, 2)]

    def mine(f, to):
        return copy(zi.at[f, c, yl, z, yh], zi.at[f, c, yl, z, yh], dev(z_=to))

    def others(f, to):
        return copy(zi.at[f, c, yl, z, oyh], zi.at[f, c, yl, z, oyh], dev(z_=to))

    y1, y02 = {}, {}
    for k in (1, 3, 0, 2):
        f = plus(z, k)
        y1[k] = copy(stage.at[f], zi.at[f, c, yl, z, yh], dev(yh_=oyh))
    ra, rb, la, lb = {}, {}, {}, {}
    for s in range(2):
        ra[s] = mine(right_f[s], zr)
        la[s] = mine(left_f[s], zl)
    for k in (1, 3, 2, 0):
        f = plus(z, k)
        here = zi.at[f, c, yl, z, yh]
        y02[k] = [copy(here, here, dev(yl_=oyl)), copy(stage.at[f], here, dev(yh_=oyh, yl_=oyl))]

    half = chunk // 2
    slab, slab_fwd = {}, []

    def slab_send(q):
        zq = plus(z, q)
        jt[zq, x] = zi[z, c, yl, zq].reshape(pair, chunk).T
        slab[q] = [copy(jt.at[zq, x], jt.at[zq, x], dev(x_=xr)), copy(jt.at[zq, x], jt.at[zq, x], dev(x_=xl))]

    def slab_forward(q):
        zq = plus(z, q)
        for cp in slab[q]:
            cp.wait_recv()
        lo, hi = pl.ds(0, half), pl.ds(half, half)
        slab_fwd.append(copy(jt.at[zq, xl, lo], jt.at[zq, xl, lo], dev(x_=xr)))
        slab_fwd.append(copy(jt.at[zq, xr, hi], jt.at[zq, xr, hi], dev(x_=xl)))

    def forward_right(f):
        ref = zi.at[f, c, yl, zl, yh]
        return copy(ref, ref, dev(z_=zr))

    def forward_left(f):
        ref = zi.at[f, c, yl, zr, oyh]
        return copy(ref, ref, dev(z_=zl))

    fr, fl = {}, {}
    shared = {}

    def share(key, ref):
        shared[key] = copy(ref, ref, dev(c_=oc))

    y1[1].wait_recv()
    rb[0] = others(right_f[0], zr)
    y1[3].wait_recv()
    lb[0] = others(left_f[0], zl)
    y1[0].wait_recv()
    slab_send(0)
    y1[2].wait_recv()
    rb[1] = others(right_f[1], zr)
    lb[1] = others(left_f[1], zl)
    ra[2] = mine(right_f[2], zr)
    la[2] = mine(left_f[2], zl)

    squares = jnp.zeros((2, cols), F32)
    for d in range(8):
        gap = stats[d, 0:2, :] * (1.0 / local_rows) - mean
        squares = squares + (stats[d, 2:4, :] + local_rows * (gap * gap))
    spread = jnp.sqrt(squares / (n_rows - 1) + DEVIATION_FLOOR)
    coefs[0:2, :] = mean
    coefs[2:4, :] = jnp.where(spread < 1.0, -(VARIANCE_WEIGHT * n_rows / (2.0 * (n_rows - 1))) / spread, 0.0)

    ra[0].wait_recv()
    rb[0].wait_recv()
    slab_send(-1)
    la[0].wait_recv()
    lb[0].wait_recv()
    slab_send(1)
    ra[1].wait_recv()
    fr[0] = forward_right(from_left_f[1])
    lb[1].wait_recv()
    fl[0] = forward_left(from_right_f[1])
    rb[2] = others(right_f[2], zr)
    lb[2] = others(left_f[2], zl)
    slab_forward(0)
    ra[3] = mine(right_f[3], zr)
    la[3] = mine(left_f[3], zl)
    fr[3] = forward_right(from_left_f[0])
    fl[1] = forward_left(from_right_f[0])
    rb[3] = others(right_f[3], zr)
    lb[3] = others(left_f[3], zl)
    rb[1].wait_recv()
    la[1].wait_recv()
    ra[2].wait_recv()
    fr[1] = forward_right(from_left_f[2])
    lb[2].wait_recv()
    fl[2] = forward_left(from_right_f[2])
    rb[2].wait_recv()
    la[2].wait_recv()

    across = {}

    def opposite(q):
        fr[q].wait_recv()
        fl[q].wait_recv()
        f = plus(z, q)
        across[q] = copy(zi.at[f, c, yl, z2], zi.at[f, c, yl, z2], dev(yl_=oyl))

    opposite(0)
    slab_send(2)
    share(("same", 0), zi.at[z, c, yl])
    slab_forward(-1)
    slab_forward(1)

    rc, lc = {}, {}
    right_c = [plus(z, k) for k in (1, 2, 3, 0)]
    left_c = [plus(z, k) for k in (3, 0, 1, 2)]
    for k in (1, 3, 2, 0):
        for cp in y02[k]:
            cp.wait_recv()
        share(("own", k), zi.at[plus(z, k), c, oyl, z])

    def direct(q):
        rc[q] = copy(zi.at[right_c[q], c, oyl, z], zi.at[right_c[q], c, oyl, z], dev(z_=zr))
        lc[q] = copy(zi.at[left_c[q], c, oyl, z], zi.at[left_c[q], c, oyl, z], dev(z_=zl))

    direct(0)
    ra[3].wait_recv()
    fr[2] = forward_right(from_left_f[3])
    lb[3].wait_recv()
    fl[3] = forward_left(from_right_f[3])
    direct(1)
    rb[3].wait_recv()
    la[3].wait_recv()
    for q in (1, 2, 3):
        opposite(q)
        share(("same", q), zi.at[plus(z, q), c, yl])
        if q == 1:
            slab_forward(2)
    direct(2)
    direct(3)

    scale = 2.0 * n_rows / (n_rows - 1.0)
    slope = scale / (n_rows - 1.0)
    edge = HUBER_EDGE * scale

    def gram(f, cc, yy, first_part, parts):
        size = parts * chunk
        g = jnp.zeros((size, chunk), F32)
        for q in range(4):
            lhs = jt[q, pl.ds(first_part, parts)].reshape(size, chunk)
            rhs = zi[f, cc, yy, q].reshape(pair, chunk)
            g = g + jnp.dot(lhs, rhs, preferred_element_type=F32)
        w = jnp.clip(g * slope, -edge, edge).astype(BF16)
        wt[f, cc, yy, pl.ds(first_part, parts)] = w.reshape(parts, chunk, chunk)

    def gram_part(cc, part):
        def body(q, carry):
            gram((z + q) % 4, cc, yl, part, 1)
            return carry

        lax.fori_loop(0, 4, body, 0)

    def gram_block(f, cc, yy):
        def body(i, carry):
            gram(f, cc, yy, 2 * i, 2)
            return carry

        lax.fori_loop(0, 2, body, 0)

    gram_part(c, x)
    for q in range(4):
        shared["same", q].wait_recv()
    gram_part(oc, x)
    row_id = lax.broadcasted_iota(jnp.int32, (chunk, chunk), 0)
    col_id = lax.broadcasted_iota(jnp.int32, (chunk, chunk), 1)
    wt[z, c, yl, x] = jnp.where(row_id == col_id, jnp.zeros((), BF16), wt[z, c, yl, x])
    for part in (xl, xr):
        gram_part(c, part)
        gram_part(oc, part)
    for cp in slab_fwd:
        cp.wait_recv()
    gram_part(c, x2)
    gram_part(oc, x2)

    def arrive(q):
        f = plus(z, q)
        rc[q].wait_recv()
        share(("left", q), zi.at[f, c, oyl, zl])
        lc[q].wait_recv()
        share(("right", q), zi.at[f, c, oyl, zr])
        across[q].wait_recv()
        share(("across", q), zi.at[f, c, oyl, z2])

    def sibling(q):
        for name in ("own", "left", "right", "across"):
            shared[name, q].wait_recv()

    for q in range(3):
        arrive(q)
        gram_block(plus(z, q), c, oyl)
        sibling(q)
        gram_block(plus(z, q), oc, oyl)
    arrive(3)
    gram(zl, c, oyl, x2, 1)
    sibling(3)
    gram(zl, oc, oyl, x2, 1)

    def product(part, k):
        zq = plus(z, k)
        acc = jnp.zeros((pair, chunk), F32)
        for f in range(4):
            for cc in range(2):
                for yy in range(2):
                    lhs = zi[f, cc, yy, zq].reshape(pair, chunk)
                    acc = acc + lax.dot_general(
                        lhs, wt[f, cc, yy, part], (((1,), (1,)), ((), ())), preferred_element_type=F32
                    )
        return acc

    def send_part(slot, value, to):
        part_out[slot] = value.astype(BF16)
        return copy(part_out.at[slot], part_in.at[slot], dev(x_=to))

    r, l = {}, {}
    r[0] = send_part(0, product(x2, 2), xr)
    l[0] = send_part(1, product(x2, 0), xl)
    r[1] = send_part(2, product(x2, 1), xr)
    l[1] = send_part(3, product(x2, 3), xl)
    for part in (xr, xl):
        gram(zl, c, oyl, part, 1)
        gram(zl, oc, oyl, part, 1)
    r[2] = send_part(4, product(xr, 0), xr)
    l[2] = send_part(5, product(xl, 2), xl)
    r[3] = send_part(6, product(xr, 3), xr)
    l[3] = send_part(7, product(xl, 1), xl)
    acc = product(xr, 2)
    r[0].wait_recv()
    r[4] = send_part(8, acc + part_in[0].astype(F32), xr)
    acc = product(xl, 0)
    l[0].wait_recv()
    l[4] = send_part(9, acc + part_in[1].astype(F32), xl)
    acc = product(xr, 1)
    r[1].wait_recv()
    r[5] = send_part(10, acc + part_in[2].astype(F32), xr)
    acc = product(xl, 3)
    l[1].wait_recv()
    l[5] = send_part(11, acc + part_in[3].astype(F32), xl)
    gram(zl, c, oyl, x, 1)
    gram(zl, oc, oyl, x, 1)

    back = []

    def give(k, total):
        zq = plus(z, k)
        rows_out[zq] = total.astype(BF16).reshape(2, local_rows, chunk)
        back.append(copy(rows_out.at[zq, oyh], rows_in.at[yh, z], dev(yh_=oyh, z_=zq)))
        if k == 0:
            rows_in[yh, z] = rows_out[z, yh]
        else:
            back.append(copy(rows_out.at[zq, yh], rows_in.at[yh, z], dev(z_=zq)))

    acc = product(x, 2)
    l[2].wait_recv()
    acc = acc + part_in[5].astype(F32)
    r[4].wait_recv()
    give(2, acc + part_in[8].astype(F32))
    acc = product(x, 0)
    r[2].wait_recv()
    acc = acc + part_in[4].astype(F32)
    l[4].wait_recv()
    give(0, acc + part_in[9].astype(F32))
    acc = product(x, 1)
    l[3].wait_recv()
    acc = acc + part_in[7].astype(F32)
    r[5].wait_recv()
    give(1, acc + part_in[10].astype(F32))
    acc = product(x, 3)
    r[3].wait_recv()
    acc = acc + part_in[6].astype(F32)
    l[5].wait_recv()
    give(3, acc + part_in[11].astype(F32))
    for cp in back:
        cp.wait_recv()
    for v in range(2):
        for f in range(4):
            cov[v, :, f * chunk : (f + 1) * chunk] = rows_in[v, f]
    for cp in sent:
        cp.wait_send()


def on_device(z_a, z_b):
    rows, cols = z_a.shape
    chunk = cols // 4
    vmem = pl.BlockSpec(memory_space=pltpu.VMEM)
    hbm = pl.BlockSpec(memory_space=pl.ANY)
    cov, coefs = pl.pallas_call(
        kernel,
        out_shape=[jax.ShapeDtypeStruct((2, rows, cols), BF16), jax.ShapeDtypeStruct((4, cols), F32)],
        in_specs=[hbm, hbm],
        out_specs=[vmem, vmem],
        scratch_shapes=[
            pltpu.VMEM((rows, cols), F32),
            pltpu.VMEM((rows, cols), F32),
            pltpu.VMEM((8, 4, cols), F32),
            pltpu.VMEM((4, 2, 2, 4, 2, rows, chunk), BF16),
            pltpu.VMEM((4, rows, chunk), BF16),
            pltpu.VMEM((4, 4, chunk, 2 * rows), BF16),
            pltpu.VMEM((4, 2, 2, 4, chunk, chunk), BF16),
            pltpu.VMEM((12, 2 * rows, chunk), BF16),
            pltpu.VMEM((12, 2 * rows, chunk), BF16),
            pltpu.VMEM((4, 2, rows, chunk), BF16),
            pltpu.VMEM((2, 4, rows, chunk), BF16),
            pltpu.SemaphoreType.DMA((2,)),
            pltpu.SemaphoreType.DMA((N_COPIES,)),
            pltpu.SemaphoreType.DMA((N_COPIES,)),
        ],
        compiler_params=pltpu.CompilerParams(collective_id=0, has_side_effects=True, vmem_limit_bytes=56 * 1024 * 1024),
        name="vicreg",
    )(z_a, z_b)
    difference = INVARIANCE_WEIGHT * (z_a - z_b)
    dz_a = difference + coefs[2:3] * (z_a - coefs[0:1]) + cov[0].astype(F32)
    dz_b = coefs[3:4] * (z_b - coefs[1:2]) - difference + cov[1].astype(F32)
    return dz_a, dz_b


def solution(mesh):
    specs = (P("dp", "mp"), P("dp", "mp"))
    return jax.shard_map(on_device, mesh=mesh, in_specs=specs, out_specs=specs, check_vma=False)
```

time: 107 us -> 96.4 us (0.901)
  Pallas kernels: 103 us -> 91.4 us
  other arithmetic: 0 us -> 2.23 us
  local copies, waits for them, and re-layouts: 2.74 us -> 0.89 us
    pallas_call x1, Pallas kernels: 103 us -> 91.4 us  [on_device(): pl.pallas_call(kernel, out_shape=[jax.ShapeDtypeStruct((2, rows, cols), B...]
    unnamed x4, local copies, waits for them, and re-layouts: 2.74 us -> 0.01 us
    add x0 -> x1, other arithmetic: none -> 2.23 us  [on_device(): dz_b = coefs[3:4] * (z_b - coefs[1:2]) - difference + cov[1].astype(F32)]
where the time goes in v2:
time: 96.4 us; the launch traced here: 95.2 us
  Pallas kernels  91.4 us (95%)
  other arithmetic  2.23 us (2%)
    pallas_call x1, Pallas kernels, on_device(): pl.pallas_call(kernel, out_shape=[jax.ShapeDtypeStruct((2, rows, cols), B...  91.4 us
    add x1, other arithmetic, on_device(): dz_b = coefs[3:4] * (z_b - coefs[1:2]) - difference + cov[1].astype(F32)  2.23 us

profile of v2, /device:TPU:0, one launch (start us, length us, event | category | flops | bytes accessed | tf_op | source)
XLA Modules:
  0.0 95.2 jit_solution(16324689779112323460)
XLA Ops:
  0.6 0.0 copy-start
  0.6 0.0 copy-start.1
  0.6 91.4 %vicreg.1 = (bf16[2,128,1024]{2,1,0:T(8,128)(2,1)}, f32[4,1024]{1,0:T(4,128)}) custom-call(f32[128,1024]{1,0:T(8,128)} %za_hbm.1, f32[128,1024]{1,0:T(8,128)} %zb_hbm.1), custom_call_target="tpu_custom_call" | custom-call | tf_op jit(solution)/shard_map/vicreg/pallas_call | solution.py:391
  92.1 0.9 fusion
  92.9 0.0 copy-done
  93.0 0.0 copy-done.1
  93.0 2.2 %convert_add_fusion = (f32[128,1024]{1,0:T(8,128)}, f32[128,1024]{1,0:T(8,128)}) fusion(f32[128,1024]{1,0:T(8,128)S(1)} %copy-done, f32[128,1024]{1,0:T(8,128)S(1)} %copy-done.1, bf16[2,128,1024]{2,1,0:T(8,128)(2,1)} %get-tuple-element.5, f32[1024]{0:T(1024)S(1)} %bitcast.11, f32[1024]{0:T(1024)S(1)} %bitcast.10, f32[1024]{0:T(1024)S(1)} %bitcast.12, ...), kind=kLoop, calls=%fused_computation | loop fusion | flops 1572864 | bytes 2637824 | tf_op jit(solution)/shard_map/add | solution.py:417
Async XLA Ops:
  0.6 92.3 %copy-start = (f32[128,1024]{1,0:T(8,128)S(1)}, f32[128,1024]{1,0:T(8,128)}, u32[]{:S(2)}) copy-start(f32[128,1024]{1,0:T(8,128)} %zb_hbm.1) | copy-start | bytes 1572868
  0.6 92.3 %copy-start.1 = (f32[128,1024]{1,0:T(8,128)S(1)}, f32[128,1024]{1,0:T(8,128)}, u32[]{:S(2)}) copy-start(f32[128,1024]{1,0:T(8,128)} %za_hbm.1) | copy-start | bytes 1572868

commit v3 on v2

--- a/solution.py
+++ b/solution.py
@@ -16,7 +16,7 @@
 N_COPIES = 128
 
 
-def kernel(za_hbm, zb_hbm, cov, coefs, za, zb, stats, zi, stage, jt, wt, part_out, part_in, rows_out, rows_in, ls, ss, rs):
+def kernel(za_hbm, zb_hbm, cov, mean_a, mean_b, pull_a, pull_b, za, zb, sums, squares, zi, stage, jt, wt, part_out, part_in, rows_out, rows_in, ls, ss, rs):
     dp = lax.axis_index("dp")
     mp = lax.axis_index("mp")
     yh, z = dp // 4, dp % 4
@@ -68,18 +68,17 @@
 
     for v, ref in enumerate((za, zb)):
         loads[v].wait()
-        total = jnp.sum(ref[...], axis=0, keepdims=True)
-        shifted = ref[...] - total * (1.0 / local_rows)
-        stats[dp, v : v + 1, :] = total
-        stats[dp, v + 2 : v + 3, :] = jnp.sum(shifted * shifted, axis=0, keepdims=True)
+        sums[dp, v : v + 1, :] = jnp.sum(ref[...], axis=0, keepdims=True)
     pl.semaphore_wait(barrier, len(partners))
-    cps = [copy(stats.at[dp], stats.at[dp], dev(yh_=peer(a, b)[0], z_=peer(a, b)[1])) for a, b in dp_peers]
-    for cp in cps:
+    def to_peers(ref):
+        return [copy(ref, ref, dev(yh_=peer(a, b)[0], z_=peer(a, b)[1])) for a, b in dp_peers]
+
+    for cp in to_peers(sums.at[dp]):
         cp.wait_recv()
 
     totals = jnp.zeros((2, cols), F32)
     for d in range(8):
-        totals = totals + stats[d, 0:2, :]
+        totals = totals + sums[d]
     mean = totals * (1.0 / n_rows)
 
     first = yh == 0
@@ -156,13 +155,10 @@
     ra[2] = mine(right_f[2], zr)
     la[2] = mine(left_f[2], zl)
 
-    squares = jnp.zeros((2, cols), F32)
-    for d in range(8):
-        gap = stats[d, 0:2, :] * (1.0 / local_rows) - mean
-        squares = squares + (stats[d, 2:4, :] + local_rows * (gap * gap))
-    spread = jnp.sqrt(squares / (n_rows - 1) + DEVIATION_FLOOR)
-    coefs[0:2, :] = mean
-    coefs[2:4, :] = jnp.where(spread < 1.0, -(VARIANCE_WEIGHT * n_rows / (2.0 * (n_rows - 1))) / spread, 0.0)
+    for v, ref in enumerate((za, zb)):
+        centered = ref[...] - mean[v : v + 1, :]
+        squares[dp, v : v + 1, :] = jnp.sum(centered * centered, axis=0, keepdims=True)
+    square_copies = to_peers(squares.at[dp])
 
     ra[0].wait_recv()
     rb[0].wait_recv()
@@ -203,79 +199,62 @@
     opposite(0)
     slab_send(2)
     share(("same", 0), zi.at[z, c, yl])
-    slab_forward(-1)
-    slab_forward(1)
 
     rc, lc = {}, {}
     right_c = [plus(z, k) for k in (1, 2, 3, 0)]
     left_c = [plus(z, k) for k in (3, 0, 1, 2)]
-    for k in (1, 3, 2, 0):
+
+    def direct(q):
+        rc[q] = copy(zi.at[right_c[q], c, oyl, z], zi.at[right_c[q], c, oyl, z], dev(z_=zr))
+        lc[q] = copy(zi.at[left_c[q], c, oyl, z], zi.at[left_c[q], c, oyl, z], dev(z_=zl))
+
+    scale = 2.0 * n_rows / (n_rows - 1.0)
+    slope = scale / (n_rows - 1.0)
+    edge = HUBER_EDGE * scale
+
+    def gram(f, cc, yy, part):
+        g = jnp.zeros((chunk, chunk), F32)
+        for q in range(4):
+            g = g + jnp.dot(jt[q, part], zi[f, cc, yy, q].reshape(pair, chunk), preferred_element_type=F32)
+        wt[f, cc, yy, part] = jnp.clip(g * slope, -edge, edge).astype(BF16)
+
+    def gram_part(cc, part):
+        for q in range(4):
+            gram(plus(z, q), cc, yl, part)
+
+    def gram_block(f):
+        for cc in (c, oc):
+            for part in range(4):
+                gram(f, cc, oyl, part)
+
+    for k in (1, 3):
         for cp in y02[k]:
             cp.wait_recv()
         share(("own", k), zi.at[plus(z, k), c, oyl, z])
-
-    def direct(q):
-        rc[q] = copy(zi.at[right_c[q], c, oyl, z], zi.at[right_c[q], c, oyl, z], dev(z_=zr))
-        lc[q] = copy(zi.at[left_c[q], c, oyl, z], zi.at[left_c[q], c, oyl, z], dev(z_=zl))
-
     direct(0)
+    slab_forward(-1)
+    slab_forward(1)
     ra[3].wait_recv()
     fr[2] = forward_right(from_left_f[3])
     lb[3].wait_recv()
     fl[3] = forward_left(from_right_f[3])
+    for k in (2, 0):
+        for cp in y02[k]:
+            cp.wait_recv()
+        share(("own", k), zi.at[plus(z, k), c, oyl, z])
     direct(1)
     rb[3].wait_recv()
     la[3].wait_recv()
-    for q in (1, 2, 3):
-        opposite(q)
-        share(("same", q), zi.at[plus(z, q), c, yl])
-        if q == 1:
-            slab_forward(2)
+    gram(z, c, yl, x)
+    opposite(1)
+    share(("same", 1), zi.at[plus(z, 1), c, yl])
+    slab_forward(2)
     direct(2)
+    opposite(2)
+    share(("same", 2), zi.at[plus(z, 2), c, yl])
+    opposite(3)
+    share(("same", 3), zi.at[plus(z, 3), c, yl])
     direct(3)
-
-    scale = 2.0 * n_rows / (n_rows - 1.0)
-    slope = scale / (n_rows - 1.0)
-    edge = HUBER_EDGE * scale
-
-    def gram(f, cc, yy, first_part, parts):
-        size = parts * chunk
-        g = jnp.zeros((size, chunk), F32)
-        for q in range(4):
-            lhs = jt[q, pl.ds(first_part, parts)].reshape(size, chunk)
-            rhs = zi[f, cc, yy, q].reshape(pair, chunk)
-            g = g + jnp.dot(lhs, rhs, preferred_element_type=F32)
-        w = jnp.clip(g * slope, -edge, edge).astype(BF16)
-        wt[f, cc, yy, pl.ds(first_part, parts)] = w.reshape(parts, chunk, chunk)
-
-    def gram_part(cc, part):
-        def body(q, carry):
-            gram((z + q) % 4, cc, yl, part, 1)
-            return carry
-
-        lax.fori_loop(0, 4, body, 0)
-
-    def gram_block(f, cc, yy):
-        def body(i, carry):
-            gram(f, cc, yy, 2 * i, 2)
-            return carry
-
-        lax.fori_loop(0, 2, body, 0)
-
-    gram_part(c, x)
-    for q in range(4):
-        shared["same", q].wait_recv()
-    gram_part(oc, x)
-    row_id = lax.broadcasted_iota(jnp.int32, (chunk, chunk), 0)
-    col_id = lax.broadcasted_iota(jnp.int32, (chunk, chunk), 1)
-    wt[z, c, yl, x] = jnp.where(row_id == col_id, jnp.zeros((), BF16), wt[z, c, yl, x])
-    for part in (xl, xr):
-        gram_part(c, part)
-        gram_part(oc, part)
-    for cp in slab_fwd:
-        cp.wait_recv()
-    gram_part(c, x2)
-    gram_part(oc, x2)
 
     def arrive(q):
         f = plus(z, q)
@@ -290,15 +269,45 @@
         for name in ("own", "left", "right", "across"):
             shared[name, q].wait_recv()
 
-    for q in range(3):
-        arrive(q)
-        gram_block(plus(z, q), c, oyl)
-        sibling(q)
-        gram_block(plus(z, q), oc, oyl)
+    for q in (1, 2, 3):
+        gram(plus(z, q), c, yl, x)
+    gram_part(c, xl)
+    gram_part(c, xr)
+    arrive(0)
+    for q in range(4):
+        shared["same", q].wait_recv()
+    gram_part(oc, x)
+    gram_part(oc, xl)
+    gram_part(oc, xr)
+    row_id = lax.broadcasted_iota(jnp.int32, (chunk, chunk), 0)
+    col_id = lax.broadcasted_iota(jnp.int32, (chunk, chunk), 1)
+    wt[z, c, yl, x] = jnp.where(row_id == col_id, jnp.zeros((), BF16), wt[z, c, yl, x])
+    arrive(1)
+    for cp in slab_fwd:
+        cp.wait_recv()
+    gram_part(c, x2)
+    gram_part(oc, x2)
+    sibling(0)
+    gram_block(z)
+    arrive(2)
+    sibling(1)
+    gram_block(zr)
     arrive(3)
-    gram(zl, c, oyl, x2, 1)
+    sibling(2)
+    gram_block(z2)
+    gram(zl, c, oyl, x2)
     sibling(3)
-    gram(zl, oc, oyl, x2, 1)
+    gram(zl, oc, oyl, x2)
+
+    for cp in square_copies:
+        cp.wait_recv()
+    variance = jnp.zeros((2, cols), F32)
+    for d in range(8):
+        variance = variance + squares[d]
+    spread = jnp.sqrt(variance / (n_rows - 1) + DEVIATION_FLOOR)
+    pull = jnp.where(spread < 1.0, -(VARIANCE_WEIGHT * n_rows / (2.0 * (n_rows - 1))) / spread, 0.0)
+    mean_a[...], mean_b[...] = mean[0:1, :], mean[1:2, :]
+    pull_a[...], pull_b[...] = pull[0:1, :], pull[1:2, :]
 
     def product(part, k):
         zq = plus(z, k)
@@ -322,8 +331,8 @@
     r[1] = send_part(2, product(x2, 1), xr)
     l[1] = send_part(3, product(x2, 3), xl)
     for part in (xr, xl):
-        gram(zl, c, oyl, part, 1)
-        gram(zl, oc, oyl, part, 1)
+        gram(zl, c, oyl, part)
+        gram(zl, oc, oyl, part)
     r[2] = send_part(4, product(xr, 0), xr)
     l[2] = send_part(5, product(xl, 2), xl)
     r[3] = send_part(6, product(xr, 3), xr)
@@ -340,8 +349,8 @@
     acc = product(xl, 3)
     l[1].wait_recv()
     l[5] = send_part(11, acc + part_in[3].astype(F32), xl)
-    gram(zl, c, oyl, x, 1)
-    gram(zl, oc, oyl, x, 1)
+    gram(zl, c, oyl, x)
+    gram(zl, oc, oyl, x)
 
     back = []
 
@@ -388,15 +397,16 @@
     chunk = cols // 4
     vmem = pl.BlockSpec(memory_space=pltpu.VMEM)
     hbm = pl.BlockSpec(memory_space=pl.ANY)
-    cov, coefs = pl.pallas_call(
+    cov, mean_a, mean_b, pull_a, pull_b = pl.pallas_call(
         kernel,
-        out_shape=[jax.ShapeDtypeStruct((2, rows, cols), BF16), jax.ShapeDtypeStruct((4, cols), F32)],
+        out_shape=[jax.ShapeDtypeStruct((2, rows, cols), BF16), *[jax.ShapeDtypeStruct((1, cols), F32)] * 4],
         in_specs=[hbm, hbm],
-        out_specs=[vmem, vmem],
+        out_specs=[vmem] * 5,
         scratch_shapes=[
             pltpu.VMEM((rows, cols), F32),
             pltpu.VMEM((rows, cols), F32),
-            pltpu.VMEM((8, 4, cols), F32),
+            pltpu.VMEM((8, 2, cols), F32),
+            pltpu.VMEM((8, 2, cols), F32),
             pltpu.VMEM((4, 2, 2, 4, 2, rows, chunk), BF16),
             pltpu.VMEM((4, rows, chunk), BF16),
             pltpu.VMEM((4, 4, chunk, 2 * rows), BF16),
@@ -413,8 +423,8 @@
         name="vicreg",
     )(z_a, z_b)
     difference = INVARIANCE_WEIGHT * (z_a - z_b)
-    dz_a = difference + coefs[2:3] * (z_a - coefs[0:1]) + cov[0].astype(F32)
-    dz_b = coefs[3:4] * (z_b - coefs[1:2]) - difference + cov[1].astype(F32)
+    dz_a = difference + pull_a * (z_a - mean_a) + cov[0].astype(F32)
+    dz_b = pull_b * (z_b - mean_b) - difference + cov[1].astype(F32)
     return dz_a, dz_b
 
 

time: 96.4 us -> 86.2 us (0.89)
  Pallas kernels: 91.4 us -> 81.5 us
    pallas_call x1, Pallas kernels: 91.4 us -> 81.5 us  [on_device(): pl.pallas_call(kernel, out_shape=[jax.ShapeDtypeStruct((2, rows, cols), B...]
where the time goes in v3:
time: 86.2 us; the launch traced here: 85.1 us
  Pallas kernels  81.5 us (95%)
  other arithmetic  2.23 us (3%)
    pallas_call x1, Pallas kernels, on_device(): pl.pallas_call(kernel, out_shape=[jax.ShapeDtypeStruct((2, rows, cols), B...  81.5 us
    add x1, other arithmetic, on_device(): dz_b = pull_b * (z_b - mean_b) - difference + cov[1].astype(F32)  2.23 us

profile of v3, /device:TPU:0, one launch (start us, length us, event | category | flops | bytes accessed | tf_op | source)
XLA Modules:
  0.0 85.1 jit_solution(11320762518878932169)
XLA Ops:
  0.6 0.0 copy-start
  0.6 0.0 copy-start.1
  0.6 81.5 %vicreg.1 = (bf16[2,128,1024]{2,1,0:T(8,128)(2,1)}, f32[1,1024]{1,0:T(1,128)}, f32[1,1024]{1,0:T(1,128)}, f32[1,1024]{1,0:T(1,128)}, f32[1,1024]{1,0:T(1,128)}) custom-call(f32[128,1024]{1,0:T(8,128)} %za_hbm.1, f32[128,1024]{1,0:T(8,128)} %zb_hbm.1), custom_call_target="tpu_custom_call" | custom-call | tf_op jit(solution)/shard_map/vicreg/pallas_call | solution.py:400
  82.2 0.0 copy-start.5
  82.2 0.0 copy-start.4
  82.2 0.0 copy-start.3
  82.2 0.0 copy-start.2
  82.2 0.0 copy-done
  82.2 0.0 copy-done.1
  82.2 0.6 copy-done.5
  82.8 0.0 copy-done.4
  82.9 0.0 copy-done.3
  82.9 0.0 copy-done.2
  82.9 2.2 %convert_add_fusion = (f32[128,1024]{1,0:T(8,128)}, f32[128,1024]{1,0:T(8,128)}) fusion(f32[128,1024]{1,0:T(8,128)S(1)} %copy-done, f32[128,1024]{1,0:T(8,128)S(1)} %copy-done.1, bf16[2,128,1024]{2,1,0:T(8,128)(2,1)} %get-tuple-element.9, f32[1024]{0:T(1024)S(1)} %bitcast.11, f32[1024]{0:T(1024)S(1)} %bitcast.13, f32[1024]{0:T(1024)S(1)} %bitcast.10, ...), kind=kLoop, calls=%fused_computation | loop fusion | flops 1572864 | bytes 2637824 | tf_op jit(solution)/shard_map/add | solution.py:427
Async XLA Ops:
  0.6 81.6 %copy-start = (f32[128,1024]{1,0:T(8,128)S(1)}, f32[128,1024]{1,0:T(8,128)}, u32[]{:S(2)}) copy-start(f32[128,1024]{1,0:T(8,128)} %zb_hbm.1) | copy-start | bytes 1572868
  0.6 81.6 %copy-start.1 = (f32[128,1024]{1,0:T(8,128)S(1)}, f32[128,1024]{1,0:T(8,128)}, u32[]{:S(2)}) copy-start(f32[128,1024]{1,0:T(8,128)} %za_hbm.1) | copy-start | bytes 1572868
  82.2 0.7 copy-start.5
  82.2 0.7 copy-start.4
  82.2 0.7 copy-start.3
  82.2 0.7 copy-start.2

commit v4 on v3

--- a/solution.py
+++ b/solution.py
@@ -16,7 +16,7 @@
 N_COPIES = 128
 
 
-def kernel(za_hbm, zb_hbm, cov, mean_a, mean_b, pull_a, pull_b, za, zb, sums, squares, zi, stage, jt, wt, part_out, part_in, rows_out, rows_in, ls, ss, rs):
+def kernel(za_hbm, zb_hbm, cov, mean_a, mean_b, pull_a, pull_b, za, zb, sums, squares, zi, stage, jt, wt, part_out, part_in, own, rows_out, rows_in, ls, ss, rs):
     dp = lax.axis_index("dp")
     mp = lax.axis_index("mp")
     yh, z = dp // 4, dp % 4
@@ -105,13 +105,18 @@
         f = plus(z, k)
         y1[k] = copy(stage.at[f], zi.at[f, c, yl, z, yh], dev(yh_=oyh))
     ra, rb, la, lb = {}, {}, {}, {}
-    for s in range(2):
+    for s in range(4):
         ra[s] = mine(right_f[s], zr)
         la[s] = mine(left_f[s], zl)
     for k in (1, 3, 2, 0):
         f = plus(z, k)
         here = zi.at[f, c, yl, z, yh]
         y02[k] = [copy(here, here, dev(yl_=oyl)), copy(stage.at[f], here, dev(yh_=oyh, yl_=oyl))]
+
+    for v, ref in enumerate((za, zb)):
+        centered = ref[...] - mean[v : v + 1, :]
+        squares[dp, v : v + 1, :] = jnp.sum(centered * centered, axis=0, keepdims=True)
+    square_copies = to_peers(squares.at[dp])
 
     half = chunk // 2
     slab, slab_fwd = {}, []
@@ -145,6 +150,8 @@
 
     y1[1].wait_recv()
     rb[0] = others(right_f[0], zr)
+    ra[1].wait_recv()
+    fr[0] = forward_right(from_left_f[1])
     y1[3].wait_recv()
     lb[0] = others(left_f[0], zl)
     y1[0].wait_recv()
@@ -152,41 +159,30 @@
     y1[2].wait_recv()
     rb[1] = others(right_f[1], zr)
     lb[1] = others(left_f[1], zl)
-    ra[2] = mine(right_f[2], zr)
-    la[2] = mine(left_f[2], zl)
-
-    for v, ref in enumerate((za, zb)):
-        centered = ref[...] - mean[v : v + 1, :]
-        squares[dp, v : v + 1, :] = jnp.sum(centered * centered, axis=0, keepdims=True)
-    square_copies = to_peers(squares.at[dp])
-
+    lb[2] = others(left_f[2], zl)
+    ra[2].wait_recv()
+    fr[1] = forward_right(from_left_f[2])
     ra[0].wait_recv()
     rb[0].wait_recv()
     slab_send(-1)
     la[0].wait_recv()
     lb[0].wait_recv()
     slab_send(1)
-    ra[1].wait_recv()
-    fr[0] = forward_right(from_left_f[1])
     lb[1].wait_recv()
     fl[0] = forward_left(from_right_f[1])
+    lb[3] = others(left_f[3], zl)
+    ra[3].wait_recv()
+    fr[2] = forward_right(from_left_f[3])
+    fl[1] = forward_left(from_right_f[0])
+    fr[3] = forward_right(from_left_f[0])
     rb[2] = others(right_f[2], zr)
-    lb[2] = others(left_f[2], zl)
-    slab_forward(0)
-    ra[3] = mine(right_f[3], zr)
-    la[3] = mine(left_f[3], zl)
-    fr[3] = forward_right(from_left_f[0])
-    fl[1] = forward_left(from_right_f[0])
     rb[3] = others(right_f[3], zr)
-    lb[3] = others(left_f[3], zl)
-    rb[1].wait_recv()
-    la[1].wait_recv()
-    ra[2].wait_recv()
-    fr[1] = forward_right(from_left_f[2])
     lb[2].wait_recv()
     fl[2] = forward_left(from_right_f[2])
-    rb[2].wait_recv()
-    la[2].wait_recv()
+    slab_forward(0)
+    for s in range(1, 4):
+        la[s].wait_recv()
+    rb[1].wait_recv()
 
     across = {}
 
@@ -227,6 +223,8 @@
             for part in range(4):
                 gram(f, cc, oyl, part)
 
+    lb[3].wait_recv()
+    fl[3] = forward_left(from_right_f[3])
     for k in (1, 3):
         for cp in y02[k]:
             cp.wait_recv()
@@ -234,24 +232,23 @@
     direct(0)
     slab_forward(-1)
     slab_forward(1)
-    ra[3].wait_recv()
-    fr[2] = forward_right(from_left_f[3])
-    lb[3].wait_recv()
-    fl[3] = forward_left(from_right_f[3])
     for k in (2, 0):
         for cp in y02[k]:
             cp.wait_recv()
         share(("own", k), zi.at[plus(z, k), c, oyl, z])
     direct(1)
+    opposite(1)
+    rb[2].wait_recv()
     rb[3].wait_recv()
-    la[3].wait_recv()
+    share(("same", 1), zi.at[plus(z, 1), c, yl])
+    shared["same", 0].wait_recv()
     gram(z, c, yl, x)
-    opposite(1)
-    share(("same", 1), zi.at[plus(z, 1), c, yl])
+    gram(z, oc, yl, x)
+    gram(zr, c, yl, x)
+    opposite(2)
+    share(("same", 2), zi.at[plus(z, 2), c, yl])
     slab_forward(2)
     direct(2)
-    opposite(2)
-    share(("same", 2), zi.at[plus(z, 2), c, yl])
     opposite(3)
     share(("same", 3), zi.at[plus(z, 3), c, yl])
     direct(3)
@@ -269,25 +266,26 @@
         for name in ("own", "left", "right", "across"):
             shared[name, q].wait_recv()
 
-    for q in (1, 2, 3):
-        gram(plus(z, q), c, yl, x)
+    gram(z2, c, yl, x)
+    gram(zl, c, yl, x)
     gram_part(c, xl)
     gram_part(c, xr)
     arrive(0)
-    for q in range(4):
+    for q in range(1, 4):
         shared["same", q].wait_recv()
-    gram_part(oc, x)
+    for q in range(1, 4):
+        gram(plus(z, q), oc, yl, x)
     gram_part(oc, xl)
     gram_part(oc, xr)
     row_id = lax.broadcasted_iota(jnp.int32, (chunk, chunk), 0)
     col_id = lax.broadcasted_iota(jnp.int32, (chunk, chunk), 1)
     wt[z, c, yl, x] = jnp.where(row_id == col_id, jnp.zeros((), BF16), wt[z, c, yl, x])
     arrive(1)
+    sibling(0)
     for cp in slab_fwd:
         cp.wait_recv()
     gram_part(c, x2)
     gram_part(oc, x2)
-    sibling(0)
     gram_block(z)
     arrive(2)
     sibling(1)
@@ -295,9 +293,54 @@
     arrive(3)
     sibling(2)
     gram_block(z2)
+    sibling(3)
     gram(zl, c, oyl, x2)
-    sibling(3)
     gram(zl, oc, oyl, x2)
+
+    def products(part_a, k_a, part_b, k_b):
+        a = b = jnp.zeros((pair, chunk), F32)
+        for f in range(4):
+            for cc in range(2):
+                for yy in range(2):
+                    a = a + lax.dot_general(
+                        zi[f, cc, yy, plus(z, k_a)].reshape(pair, chunk),
+                        wt[f, cc, yy, part_a],
+                        (((1,), (1,)), ((), ())),
+                        preferred_element_type=F32,
+                    )
+                    b = b + lax.dot_general(
+                        zi[f, cc, yy, plus(z, k_b)].reshape(pair, chunk),
+                        wt[f, cc, yy, part_b],
+                        (((1,), (1,)), ((), ())),
+                        preferred_element_type=F32,
+                    )
+        return a, b
+
+    def send_parts(slot, a, b):
+        part_out[slot] = a.astype(BF16)
+        part_out[slot + 1] = b.astype(BF16)
+        right = copy(part_out.at[slot], part_in.at[slot], dev(x_=xr))
+        left = copy(part_out.at[slot + 1], part_in.at[slot + 1], dev(x_=xl))
+        return right, left
+
+    r, l = {}, {}
+    r[0], l[0] = send_parts(0, *products(x2, 2, x2, 0))
+    r[1], l[1] = send_parts(2, *products(x2, 1, x2, 3))
+    for part in (xr, xl):
+        gram(zl, c, oyl, part)
+        gram(zl, oc, oyl, part)
+    r[2], l[2] = send_parts(4, *products(xr, 0, xl, 2))
+    r[3], l[3] = send_parts(6, *products(xr, 3, xl, 1))
+    a, b = products(xr, 2, xl, 0)
+    r[0].wait_recv()
+    l[0].wait_recv()
+    r[4], l[4] = send_parts(8, a + part_in[0].astype(F32), b + part_in[1].astype(F32))
+    a, b = products(xr, 1, xl, 3)
+    r[1].wait_recv()
+    l[1].wait_recv()
+    r[5], l[5] = send_parts(10, a + part_in[2].astype(F32), b + part_in[3].astype(F32))
+    gram(zl, c, oyl, x)
+    gram(zl, oc, oyl, x)
 
     for cp in square_copies:
         cp.wait_recv()
@@ -309,49 +352,6 @@
     mean_a[...], mean_b[...] = mean[0:1, :], mean[1:2, :]
     pull_a[...], pull_b[...] = pull[0:1, :], pull[1:2, :]
 
-    def product(part, k):
-        zq = plus(z, k)
-        acc = jnp.zeros((pair, chunk), F32)
-        for f in range(4):
-            for cc in range(2):
-                for yy in range(2):
-                    lhs = zi[f, cc, yy, zq].reshape(pair, chunk)
-                    acc = acc + lax.dot_general(
-                        lhs, wt[f, cc, yy, part], (((1,), (1,)), ((), ())), preferred_element_type=F32
-                    )
-        return acc
-
-    def send_part(slot, value, to):
-        part_out[slot] = value.astype(BF16)
-        return copy(part_out.at[slot], part_in.at[slot], dev(x_=to))
-
-    r, l = {}, {}
-    r[0] = send_part(0, product(x2, 2), xr)
-    l[0] = send_part(1, product(x2, 0), xl)
-    r[1] = send_part(2, product(x2, 1), xr)
-    l[1] = send_part(3, product(x2, 3), xl)
-    for part in (xr, xl):
-        gram(zl, c, oyl, part)
-        gram(zl, oc, oyl, part)
-    r[2] = send_part(4, product(xr, 0), xr)
-    l[2] = send_part(5, product(xl, 2), xl)
-    r[3] = send_part(6, product(xr, 3), xr)
-    l[3] = send_part(7, product(xl, 1), xl)
-    acc = product(xr, 2)
-    r[0].wait_recv()
-    r[4] = send_part(8, acc + part_in[0].astype(F32), xr)
-    acc = product(xl, 0)
-    l[0].wait_recv()
-    l[4] = send_part(9, acc + part_in[1].astype(F32), xl)
-    acc = product(xr, 1)
-    r[1].wait_recv()
-    r[5] = send_part(10, acc + part_in[2].astype(F32), xr)
-    acc = product(xl, 3)
-    l[1].wait_recv()
-    l[5] = send_part(11, acc + part_in[3].astype(F32), xl)
-    gram(zl, c, oyl, x)
-    gram(zl, oc, oyl, x)
-
     back = []
 
     def give(k, total):
@@ -363,26 +363,22 @@
         else:
             back.append(copy(rows_out.at[zq, yh], rows_in.at[yh, z], dev(z_=zq)))
 
-    acc = product(x, 2)
+    a, b = products(x, 2, x, 0)
+    own[0], own[1] = a, b
+    a, b = products(x, 1, x, 3)
+    own[2], own[3] = a, b
     l[2].wait_recv()
-    acc = acc + part_in[5].astype(F32)
     r[4].wait_recv()
-    give(2, acc + part_in[8].astype(F32))
-    acc = product(x, 0)
+    give(2, own[0] + (part_in[5].astype(F32) + part_in[8].astype(F32)))
     r[2].wait_recv()
-    acc = acc + part_in[4].astype(F32)
     l[4].wait_recv()
-    give(0, acc + part_in[9].astype(F32))
-    acc = product(x, 1)
+    give(0, own[1] + (part_in[4].astype(F32) + part_in[9].astype(F32)))
     l[3].wait_recv()
-    acc = acc + part_in[7].astype(F32)
     r[5].wait_recv()
-    give(1, acc + part_in[10].astype(F32))
-    acc = product(x, 3)
+    give(1, own[2] + (part_in[7].astype(F32) + part_in[10].astype(F32)))
     r[3].wait_recv()
-    acc = acc + part_in[6].astype(F32)
     l[5].wait_recv()
-    give(3, acc + part_in[11].astype(F32))
+    give(3, own[3] + (part_in[6].astype(F32) + part_in[11].astype(F32)))
     for cp in back:
         cp.wait_recv()
     for v in range(2):
@@ -413,6 +409,7 @@
             pltpu.VMEM((4, 2, 2, 4, chunk, chunk), BF16),
             pltpu.VMEM((12, 2 * rows, chunk), BF16),
             pltpu.VMEM((12, 2 * rows, chunk), BF16),
+            pltpu.VMEM((4, 2 * rows, chunk), F32),
             pltpu.VMEM((4, 2, rows, chunk), BF16),
             pltpu.VMEM((2, 4, rows, chunk), BF16),
             pltpu.SemaphoreType.DMA((2,)),

time: 86.2 us -> 80.6 us (0.935)
  Pallas kernels: 81.5 us -> 76.1 us
    pallas_call x1, Pallas kernels: 81.5 us -> 76.1 us  [on_device(): pl.pallas_call(kernel, out_shape=[jax.ShapeDtypeStruct((2, rows, cols), B...]
where the time goes in v4:
time: 80.6 us; the launch traced here: 79.7 us
  Pallas kernels  76.1 us (94%)
  other arithmetic  2.23 us (3%)
    pallas_call x1, Pallas kernels, on_device(): pl.pallas_call(kernel, out_shape=[jax.ShapeDtypeStruct((2, rows, cols), B...  76.1 us
    add x1, other arithmetic, on_device(): dz_b = pull_b * (z_b - mean_b) - difference + cov[1].astype(F32)  2.23 us

profile of v4, /device:TPU:0, one launch (start us, length us, event | category | flops | bytes accessed | tf_op | source)
XLA Modules:
  0.0 79.7 jit_solution(498738282038117661)
XLA Ops:
  0.6 0.0 copy-start
  0.6 0.0 copy-start.1
  0.6 76.1 %vicreg.1 = (bf16[2,128,1024]{2,1,0:T(8,128)(2,1)}, f32[1,1024]{1,0:T(1,128)}, f32[1,1024]{1,0:T(1,128)}, f32[1,1024]{1,0:T(1,128)}, f32[1,1024]{1,0:T(1,128)}) custom-call(f32[128,1024]{1,0:T(8,128)} %za_hbm.1, f32[128,1024]{1,0:T(8,128)} %zb_hbm.1), custom_call_target="tpu_custom_call" | custom-call | tf_op jit(solution)/shard_map/vicreg/pallas_call | solution.py:396
  76.8 0.0 copy-start.5
  76.8 0.0 copy-start.4
  76.8 0.0 copy-start.3
  76.8 0.0 copy-start.2
  76.8 0.0 copy-done
  76.8 0.0 copy-done.1
  76.8 0.6 copy-done.5
  77.5 0.0 copy-done.4
  77.5 0.0 copy-done.3
  77.5 0.0 copy-done.2
  77.5 2.2 %convert_add_fusion = (f32[128,1024]{1,0:T(8,128)}, f32[128,1024]{1,0:T(8,128)}) fusion(f32[128,1024]{1,0:T(8,128)S(1)} %copy-done, f32[128,1024]{1,0:T(8,128)S(1)} %copy-done.1, bf16[2,128,1024]{2,1,0:T(8,128)(2,1)} %get-tuple-element.9, f32[1024]{0:T(1024)S(1)} %bitcast.11, f32[1024]{0:T(1024)S(1)} %bitcast.13, f32[1024]{0:T(1024)S(1)} %bitcast.10, ...), kind=kLoop, calls=%fused_computation | loop fusion | flops 1572864 | bytes 2637824 | tf_op jit(solution)/shard_map/add | solution.py:424
Async XLA Ops:
  0.6 76.2 %copy-start = (f32[128,1024]{1,0:T(8,128)S(1)}, f32[128,1024]{1,0:T(8,128)}, u32[]{:S(2)}) copy-start(f32[128,1024]{1,0:T(8,128)} %zb_hbm.1) | copy-start | bytes 1572868
  0.6 76.2 %copy-start.1 = (f32[128,1024]{1,0:T(8,128)S(1)}, f32[128,1024]{1,0:T(8,128)}, u32[]{:S(2)}) copy-start(f32[128,1024]{1,0:T(8,128)} %za_hbm.1) | copy-start | bytes 1572868
  76.8 0.7 copy-start.5
  76.8 0.7 copy-start.4
  76.8 0.7 copy-start.3
  76.8 0.7 copy-start.2

commit v5 on v4

--- a/solution.py
+++ b/solution.py
@@ -101,7 +101,7 @@
         return copy(zi.at[f, c, yl, z, oyh], zi.at[f, c, yl, z, oyh], dev(z_=to))
 
     y1, y02 = {}, {}
-    for k in (1, 3, 0, 2):
+    for k in (0, 1, 3, 2):
         f = plus(z, k)
         y1[k] = copy(stage.at[f], zi.at[f, c, yl, z, yh], dev(yh_=oyh))
     ra, rb, la, lb = {}, {}, {}, {}
@@ -148,14 +148,14 @@
     def share(key, ref):
         shared[key] = copy(ref, ref, dev(c_=oc))
 
+    y1[0].wait_recv()
+    slab_send(0)
     y1[1].wait_recv()
     rb[0] = others(right_f[0], zr)
     ra[1].wait_recv()
     fr[0] = forward_right(from_left_f[1])
     y1[3].wait_recv()
     lb[0] = others(left_f[0], zl)
-    y1[0].wait_recv()
-    slab_send(0)
     y1[2].wait_recv()
     rb[1] = others(right_f[1], zr)
     lb[1] = others(left_f[1], zl)
@@ -218,11 +218,6 @@
         for q in range(4):
             gram(plus(z, q), cc, yl, part)
 
-    def gram_block(f):
-        for cc in (c, oc):
-            for part in range(4):
-                gram(f, cc, oyl, part)
-
     lb[3].wait_recv()
     fl[3] = forward_left(from_right_f[3])
     for k in (1, 3):
@@ -240,17 +235,17 @@
     opposite(1)
     rb[2].wait_recv()
     rb[3].wait_recv()
-    share(("same", 1), zi.at[plus(z, 1), c, yl])
+    share(("same", 1), zi.at[zr, c, yl])
     shared["same", 0].wait_recv()
     gram(z, c, yl, x)
     gram(z, oc, yl, x)
     gram(zr, c, yl, x)
     opposite(2)
-    share(("same", 2), zi.at[plus(z, 2), c, yl])
+    share(("same", 2), zi.at[z2, c, yl])
     slab_forward(2)
     direct(2)
     opposite(3)
-    share(("same", 3), zi.at[plus(z, 3), c, yl])
+    share(("same", 3), zi.at[zl, c, yl])
     direct(3)
 
     def arrive(q):
@@ -284,18 +279,24 @@
     sibling(0)
     for cp in slab_fwd:
         cp.wait_recv()
+
+    def gram_other(q, parts):
+        for part in parts:
+            for cc in (c, oc):
+                gram(plus(z, q), cc, oyl, part)
+
     gram_part(c, x2)
     gram_part(oc, x2)
-    gram_block(z)
+    gram_other(0, (x2, xl, xr))
     arrive(2)
     sibling(1)
-    gram_block(zr)
+    sibling(2)
+    gram_other(1, (x2,))
+    gram_other(2, (x2,))
     arrive(3)
-    sibling(2)
-    gram_block(z2)
+    gram_other(1, (xl, xr))
     sibling(3)
-    gram(zl, c, oyl, x2)
-    gram(zl, oc, oyl, x2)
+    gram_other(3, (x2,))
 
     def products(part_a, k_a, part_b, k_b):
         a = b = jnp.zeros((pair, chunk), F32)
@@ -326,9 +327,8 @@
     r, l = {}, {}
     r[0], l[0] = send_parts(0, *products(x2, 2, x2, 0))
     r[1], l[1] = send_parts(2, *products(x2, 1, x2, 3))
-    for part in (xr, xl):
-        gram(zl, c, oyl, part)
-        gram(zl, oc, oyl, part)
+    gram_other(2, (xl, xr))
+    gram_other(3, (xl, xr))
     r[2], l[2] = send_parts(4, *products(xr, 0, xl, 2))
     r[3], l[3] = send_parts(6, *products(xr, 3, xl, 1))
     a, b = products(xr, 2, xl, 0)
@@ -339,8 +339,8 @@
     r[1].wait_recv()
     l[1].wait_recv()
     r[5], l[5] = send_parts(10, a + part_in[2].astype(F32), b + part_in[3].astype(F32))
-    gram(zl, c, oyl, x)
-    gram(zl, oc, oyl, x)
+    for q in range(4):
+        gram_other(q, (x,))
 
     for cp in square_copies:
         cp.wait_recv()

time: 80.6 us -> 79.9 us (level)
  no operation moved by 1% of the time
where the time goes in v5:
time: 79.9 us; the launch traced here: 79.7 us
  Pallas kernels  76.2 us (95%)
  other arithmetic  2.23 us (3%)
    pallas_call x1, Pallas kernels, on_device(): pl.pallas_call(kernel, out_shape=[jax.ShapeDtypeStruct((2, rows, cols), B...  76.2 us
    add x1, other arithmetic, on_device(): dz_b = pull_b * (z_b - mean_b) - difference + cov[1].astype(F32)  2.23 us

profile of v5, /device:TPU:0, one launch (start us, length us, event | category | flops | bytes accessed | tf_op | source)
XLA Modules:
  0.0 79.7 jit_solution(9361213434207761996)
XLA Ops:
  0.6 0.0 copy-start
  0.6 0.0 copy-start.1
  0.6 76.2 %vicreg.1 = (bf16[2,128,1024]{2,1,0:T(8,128)(2,1)}, f32[1,1024]{1,0:T(1,128)}, f32[1,1024]{1,0:T(1,128)}, f32[1,1024]{1,0:T(1,128)}, f32[1,1024]{1,0:T(1,128)}) custom-call(f32[128,1024]{1,0:T(8,128)} %za_hbm.1, f32[128,1024]{1,0:T(8,128)} %zb_hbm.1), custom_call_target="tpu_custom_call" | custom-call | tf_op jit(solution)/shard_map/vicreg/pallas_call | solution.py:396
  76.8 0.0 copy-start.5
  76.8 0.0 copy-start.4
  76.8 0.0 copy-start.3
  76.8 0.0 copy-start.2
  76.9 0.0 copy-done
  76.9 0.0 copy-done.1
  76.9 0.6 copy-done.5
  77.5 0.0 copy-done.4
  77.5 0.0 copy-done.3
  77.5 0.0 copy-done.2
  77.5 2.2 %convert_add_fusion = (f32[128,1024]{1,0:T(8,128)}, f32[128,1024]{1,0:T(8,128)}) fusion(f32[128,1024]{1,0:T(8,128)S(1)} %copy-done, f32[128,1024]{1,0:T(8,128)S(1)} %copy-done.1, bf16[2,128,1024]{2,1,0:T(8,128)(2,1)} %get-tuple-element.9, f32[1024]{0:T(1024)S(1)} %bitcast.11, f32[1024]{0:T(1024)S(1)} %bitcast.13, f32[1024]{0:T(1024)S(1)} %bitcast.10, ...), kind=kLoop, calls=%fused_computation | loop fusion | flops 1572864 | bytes 2637824 | tf_op jit(solution)/shard_map/add | solution.py:424
Async XLA Ops:
  0.6 76.2 %copy-start = (f32[128,1024]{1,0:T(8,128)S(1)}, f32[128,1024]{1,0:T(8,128)}, u32[]{:S(2)}) copy-start(f32[128,1024]{1,0:T(8,128)} %zb_hbm.1) | copy-start | bytes 1572868
  0.6 76.2 %copy-start.1 = (f32[128,1024]{1,0:T(8,128)S(1)}, f32[128,1024]{1,0:T(8,128)}, u32[]{:S(2)}) copy-start(f32[128,1024]{1,0:T(8,128)} %za_hbm.1) | copy-start | bytes 1572868
  76.8 0.7 copy-start.5
  76.8 0.7 copy-start.4
  76.8 0.7 copy-start.3
  76.8 0.7 copy-start.2

commit v6 on v5

--- a/solution.py
+++ b/solution.py
@@ -13,7 +13,7 @@
 MESH = pl.DeviceIdType.MESH
 F32 = jnp.float32
 BF16 = jnp.bfloat16
-N_COPIES = 128
+N_COPIES = 136
 
 
 def kernel(za_hbm, zb_hbm, cov, mean_a, mean_b, pull_a, pull_b, za, zb, sums, squares, zi, stage, jt, wt, part_out, part_in, own, rows_out, rows_in, ls, ss, rs):
@@ -162,12 +162,29 @@
     lb[2] = others(left_f[2], zl)
     ra[2].wait_recv()
     fr[1] = forward_right(from_left_f[2])
+
+    def to_other(ref):
+        return copy(ref, ref, dev(yl_=oyl))
+
     ra[0].wait_recv()
     rb[0].wait_recv()
     slab_send(-1)
+    near_left = to_other(zi.at[z, c, yl, zl])
     la[0].wait_recv()
     lb[0].wait_recv()
     slab_send(1)
+    near_right = to_other(zi.at[z, c, yl, zr])
+    across = {q: [] for q in range(4)}
+
+    def opposite_mine(q):
+        fr[q].wait_recv()
+        across[q].append(to_other(zi.at[plus(z, q), c, yl, z2, yh]))
+
+    def opposite_others(q):
+        fl[q].wait_recv()
+        across[q].append(to_other(zi.at[plus(z, q), c, yl, z2, oyh]))
+        share(("same", q), zi.at[plus(z, q), c, yl])
+
     lb[1].wait_recv()
     fl[0] = forward_left(from_right_f[1])
     lb[3] = others(left_f[3], zl)
@@ -177,24 +194,20 @@
     fr[3] = forward_right(from_left_f[0])
     rb[2] = others(right_f[2], zr)
     rb[3] = others(right_f[3], zr)
+    opposite_mine(0)
     lb[2].wait_recv()
     fl[2] = forward_left(from_right_f[2])
     slab_forward(0)
     for s in range(1, 4):
         la[s].wait_recv()
     rb[1].wait_recv()
-
-    across = {}
-
-    def opposite(q):
-        fr[q].wait_recv()
-        fl[q].wait_recv()
-        f = plus(z, q)
-        across[q] = copy(zi.at[f, c, yl, z2], zi.at[f, c, yl, z2], dev(yl_=oyl))
-
-    opposite(0)
+    opposite_mine(1)
+    opposite_others(0)
     slab_send(2)
-    share(("same", 0), zi.at[z, c, yl])
+    lb[3].wait_recv()
+    fl[3] = forward_left(from_right_f[3])
+    opposite_mine(2)
+    opposite_mine(3)
 
     rc, lc = {}, {}
     right_c = [plus(z, k) for k in (1, 2, 3, 0)]
@@ -218,43 +231,34 @@
         for q in range(4):
             gram(plus(z, q), cc, yl, part)
 
-    lb[3].wait_recv()
-    fl[3] = forward_left(from_right_f[3])
-    for k in (1, 3):
-        for cp in y02[k]:
-            cp.wait_recv()
-        share(("own", k), zi.at[plus(z, k), c, oyl, z])
-    direct(0)
-    slab_forward(-1)
-    slab_forward(1)
-    for k in (2, 0):
+    for k in (2, 0, 3, 1):
         for cp in y02[k]:
             cp.wait_recv()
         share(("own", k), zi.at[plus(z, k), c, oyl, z])
     direct(1)
-    opposite(1)
+    slab_forward(-1)
+    slab_forward(1)
     rb[2].wait_recv()
     rb[3].wait_recv()
-    share(("same", 1), zi.at[zr, c, yl])
+    opposite_others(1)
+    direct(2)
     shared["same", 0].wait_recv()
     gram(z, c, yl, x)
     gram(z, oc, yl, x)
     gram(zr, c, yl, x)
-    opposite(2)
-    share(("same", 2), zi.at[z2, c, yl])
     slab_forward(2)
-    direct(2)
-    opposite(3)
-    share(("same", 3), zi.at[zl, c, yl])
+    opposite_others(2)
     direct(3)
+    opposite_others(3)
 
     def arrive(q):
         f = plus(z, q)
-        rc[q].wait_recv()
+        (rc[q] if q else near_left).wait_recv()
         share(("left", q), zi.at[f, c, oyl, zl])
-        lc[q].wait_recv()
+        (lc[q] if q else near_right).wait_recv()
         share(("right", q), zi.at[f, c, oyl, zr])
-        across[q].wait_recv()
+        for cp in across[q]:
+            cp.wait_recv()
         share(("across", q), zi.at[f, c, oyl, z2])
 
     def sibling(q):
@@ -287,58 +291,77 @@
 
     gram_part(c, x2)
     gram_part(oc, x2)
-    gram_other(0, (x2, xl, xr))
+    gram_other(0, (x2,))
     arrive(2)
     sibling(1)
     sibling(2)
     gram_other(1, (x2,))
     gram_other(2, (x2,))
-    arrive(3)
-    gram_other(1, (xl, xr))
-    sibling(3)
-    gram_other(3, (x2,))
-
-    def products(part_a, k_a, part_b, k_b):
-        a = b = jnp.zeros((pair, chunk), F32)
-        for f in range(4):
-            for cc in range(2):
-                for yy in range(2):
-                    a = a + lax.dot_general(
-                        zi[f, cc, yy, plus(z, k_a)].reshape(pair, chunk),
-                        wt[f, cc, yy, part_a],
-                        (((1,), (1,)), ((), ())),
-                        preferred_element_type=F32,
-                    )
-                    b = b + lax.dot_general(
-                        zi[f, cc, yy, plus(z, k_b)].reshape(pair, chunk),
-                        wt[f, cc, yy, part_b],
-                        (((1,), (1,)), ((), ())),
-                        preferred_element_type=F32,
-                    )
-        return a, b
-
-    def send_parts(slot, a, b):
-        part_out[slot] = a.astype(BF16)
-        part_out[slot + 1] = b.astype(BF16)
+
+    blocks = [(plus(z, q), cc, yy) for q in range(4) for yy in (yl, oyl) for cc in (0, 1)]
+
+    def products(tiles, over, start=None):
+        accs = [jnp.zeros((pair, chunk), F32) for _ in tiles] if start is None else start
+        for f, cc, yy in over:
+            for i, (part, k) in enumerate(tiles):
+                accs[i] = accs[i] + lax.dot_general(
+                    zi[f, cc, yy, plus(z, k)].reshape(pair, chunk),
+                    wt[f, cc, yy, part],
+                    (((1,), (1,)), ((), ())),
+                    preferred_element_type=F32,
+                )
+        return accs
+
+    def keep(slot, value):
+        part_out[slot] = value.astype(BF16).reshape(2, local_rows, chunk)
+
+    def send_parts(slot):
         right = copy(part_out.at[slot], part_in.at[slot], dev(x_=xr))
         left = copy(part_out.at[slot + 1], part_in.at[slot + 1], dev(x_=xl))
         return right, left
 
+    def send_halves(slot):
+        return [
+            [copy(part_out.at[i, p], part_in.at[i, p], dev(x_=to)) for p in (oyh, yh)]
+            for i, to in ((slot, xr), (slot + 1, xl))
+        ]
+
+    def taken(slot):
+        return part_in[slot].astype(F32).reshape(pair, chunk)
+
+    turn = [(x2, 2), (x2, 0), (x2, 1), (x2, 3)]
+    for i, acc in enumerate(products(turn, blocks[:14])):
+        own[i] = acc
+    arrive(3)
+    sibling(3)
+    gram_other(3, (x2,))
+    for i, acc in enumerate(products(turn, blocks[14:], [own[i] for i in range(4)])):
+        keep(i, acc)
     r, l = {}, {}
-    r[0], l[0] = send_parts(0, *products(x2, 2, x2, 0))
-    r[1], l[1] = send_parts(2, *products(x2, 1, x2, 3))
-    gram_other(2, (xl, xr))
-    gram_other(3, (xl, xr))
-    r[2], l[2] = send_parts(4, *products(xr, 0, xl, 2))
-    r[3], l[3] = send_parts(6, *products(xr, 3, xl, 1))
-    a, b = products(xr, 2, xl, 0)
+    r[0], l[0] = send_parts(0)
+    r[1], l[1] = send_parts(2)
+    for q in range(4):
+        gram_other(q, (xl, xr))
+    a, b = products([(xr, 0), (xl, 2)], blocks)
+    keep(4, a)
+    keep(5, b)
+    r[2], l[2] = send_parts(4)
+    a, b = products([(xr, 3), (xl, 1)], blocks)
+    keep(6, a)
+    keep(7, b)
+    r[3], l[3] = send_parts(6)
+    a, b = products([(xr, 2), (xl, 0)], blocks)
     r[0].wait_recv()
     l[0].wait_recv()
-    r[4], l[4] = send_parts(8, a + part_in[0].astype(F32), b + part_in[1].astype(F32))
-    a, b = products(xr, 1, xl, 3)
+    keep(8, a + taken(0))
+    keep(9, b + taken(1))
+    r[4], l[4] = send_halves(8)
+    a, b = products([(xr, 1), (xl, 3)], blocks)
     r[1].wait_recv()
     l[1].wait_recv()
-    r[5], l[5] = send_parts(10, a + part_in[2].astype(F32), b + part_in[3].astype(F32))
+    keep(10, a + taken(2))
+    keep(11, b + taken(3))
+    r[5], l[5] = send_halves(10)
     for q in range(4):
         gram_other(q, (x,))
 
@@ -352,33 +375,34 @@
     mean_a[...], mean_b[...] = mean[0:1, :], mean[1:2, :]
     pull_a[...], pull_b[...] = pull[0:1, :], pull[1:2, :]
 
+    for k in (2, 1):
+        a, b = products([(x, k), (x, (k + 2) % 4)], blocks)
+        own[k] = a
+        own[(k + 2) % 4] = b
     back = []
 
-    def give(k, total):
+    def give(k, which, straight, summed, far):
         zq = plus(z, k)
-        rows_out[zq] = total.astype(BF16).reshape(2, local_rows, chunk)
-        back.append(copy(rows_out.at[zq, oyh], rows_in.at[yh, z], dev(yh_=oyh, z_=zq)))
-        if k == 0:
+        p = (oyh, yh)[which]
+        far[which].wait_recv()
+        rows = pl.ds(pl.multiple_of(p * local_rows, local_rows), local_rows)
+        total = own[k, rows, :] + (part_in[straight, p].astype(F32) + part_in[summed, p].astype(F32))
+        rows_out[zq, p] = total.astype(BF16)
+        if k or not which:
+            back.append(copy(rows_out.at[zq, p], rows_in.at[yh, z], dev(yh_=p, z_=zq)))
+        else:
             rows_in[yh, z] = rows_out[z, yh]
-        else:
-            back.append(copy(rows_out.at[zq, yh], rows_in.at[yh, z], dev(z_=zq)))
-
-    a, b = products(x, 2, x, 0)
-    own[0], own[1] = a, b
-    a, b = products(x, 1, x, 3)
-    own[2], own[3] = a, b
+
     l[2].wait_recv()
-    r[4].wait_recv()
-    give(2, own[0] + (part_in[5].astype(F32) + part_in[8].astype(F32)))
     r[2].wait_recv()
-    l[4].wait_recv()
-    give(0, own[1] + (part_in[4].astype(F32) + part_in[9].astype(F32)))
+    for which in (0, 1):
+        give(2, which, 5, 8, r[4])
+        give(0, which, 4, 9, l[4])
     l[3].wait_recv()
-    r[5].wait_recv()
-    give(1, own[2] + (part_in[7].astype(F32) + part_in[10].astype(F32)))
     r[3].wait_recv()
-    l[5].wait_recv()
-    give(3, own[3] + (part_in[6].astype(F32) + part_in[11].astype(F32)))
+    for which in (0, 1):
+        give(1, which, 7, 10, r[5])
+        give(3, which, 6, 11, l[5])
     for cp in back:
         cp.wait_recv()
     for v in range(2):
@@ -407,8 +431,8 @@
             pltpu.VMEM((4, rows, chunk), BF16),
             pltpu.VMEM((4, 4, chunk, 2 * rows), BF16),
             pltpu.VMEM((4, 2, 2, 4, chunk, chunk), BF16),
-            pltpu.VMEM((12, 2 * rows, chunk), BF16),
-            pltpu.VMEM((12, 2 * rows, chunk), BF16),
+            pltpu.VMEM((12, 2, rows, chunk), BF16),
+            pltpu.VMEM((12, 2, rows, chunk), BF16),
             pltpu.VMEM((4, 2 * rows, chunk), F32),
             pltpu.VMEM((4, 2, rows, chunk), BF16),
             pltpu.VMEM((2, 4, rows, chunk), BF16),

time: 79.9 us -> 79.3 us (level)
  no operation moved by 1% of the time
where the time goes in v6:
time: 79.3 us; the launch traced here: 79.1 us
  Pallas kernels  75.5 us (95%)
  other arithmetic  2.23 us (3%)
    pallas_call x1, Pallas kernels, on_device(): pl.pallas_call(kernel, out_shape=[jax.ShapeDtypeStruct((2, rows, cols), B...  75.5 us
    add x1, other arithmetic, on_device(): dz_b = pull_b * (z_b - mean_b) - difference + cov[1].astype(F32)  2.23 us

profile of v6, /device:TPU:0, one launch (start us, length us, event | category | flops | bytes accessed | tf_op | source)
XLA Modules:
  0.0 79.1 jit_solution(6452096464465751077)
XLA Ops:
  0.6 0.0 copy-start
  0.6 0.0 copy-start.1
  0.6 75.5 %vicreg.1 = (bf16[2,128,1024]{2,1,0:T(8,128)(2,1)}, f32[1,1024]{1,0:T(1,128)}, f32[1,1024]{1,0:T(1,128)}, f32[1,1024]{1,0:T(1,128)}, f32[1,1024]{1,0:T(1,128)}) custom-call(f32[128,1024]{1,0:T(8,128)} %za_hbm.1, f32[128,1024]{1,0:T(8,128)} %zb_hbm.1), custom_call_target="tpu_custom_call" | custom-call | tf_op jit(solution)/shard_map/vicreg/pallas_call | solution.py:420
  76.2 0.0 copy-start.5
  76.2 0.0 copy-start.4
  76.2 0.0 copy-start.3
  76.2 0.0 copy-start.2
  76.2 0.0 copy-done
  76.2 0.0 copy-done.1
  76.2 0.6 copy-done.5
  76.8 0.0 copy-done.4
  76.8 0.0 copy-done.3
  76.9 0.0 copy-done.2
  76.9 2.2 %convert_add_fusion = (f32[128,1024]{1,0:T(8,128)}, f32[128,1024]{1,0:T(8,128)}) fusion(f32[128,1024]{1,0:T(8,128)S(1)} %copy-done, f32[128,1024]{1,0:T(8,128)S(1)} %copy-done.1, bf16[2,128,1024]{2,1,0:T(8,128)(2,1)} %get-tuple-element.9, f32[1024]{0:T(1024)S(1)} %bitcast.11, f32[1024]{0:T(1024)S(1)} %bitcast.13, f32[1024]{0:T(1024)S(1)} %bitcast.10, ...), kind=kLoop, calls=%fused_computation | loop fusion | flops 1572864 | bytes 2637824 | tf_op jit(solution)/shard_map/add | solution.py:448
Async XLA Ops:
  0.6 75.6 %copy-start = (f32[128,1024]{1,0:T(8,128)S(1)}, f32[128,1024]{1,0:T(8,128)}, u32[]{:S(2)}) copy-start(f32[128,1024]{1,0:T(8,128)} %zb_hbm.1) | copy-start | bytes 1572868
  0.6 75.6 %copy-start.1 = (f32[128,1024]{1,0:T(8,128)S(1)}, f32[128,1024]{1,0:T(8,128)}, u32[]{:S(2)}) copy-start(f32[128,1024]{1,0:T(8,128)} %za_hbm.1) | copy-start | bytes 1572868
  76.2 0.7 copy-start.5
  76.2 0.7 copy-start.4
  76.2 0.7 copy-start.3
  76.2 0.7 copy-start.2

commit v7 on v6

--- a/solution.py
+++ b/solution.py
@@ -249,6 +249,13 @@
     slab_forward(2)
     opposite_others(2)
     direct(3)
+    shared["same", 1].wait_recv()
+    gram(z2, c, yl, x)
+    gram(zr, oc, yl, x)
+    for part in (xl, xr):
+        gram(z, c, yl, part)
+        gram(z, oc, yl, part)
+        gram(zr, c, yl, part)
     opposite_others(3)
 
     def arrive(q):
@@ -265,21 +272,13 @@
         for name in ("own", "left", "right", "across"):
             shared[name, q].wait_recv()
 
-    gram(z2, c, yl, x)
-    gram(zl, c, yl, x)
-    gram_part(c, xl)
-    gram_part(c, xr)
+    for part in (xl, xr):
+        gram(z2, c, yl, part)
+        gram(zl, c, yl, part)
     arrive(0)
-    for q in range(1, 4):
+    arrive(1)
+    for q in (2, 3):
         shared["same", q].wait_recv()
-    for q in range(1, 4):
-        gram(plus(z, q), oc, yl, x)
-    gram_part(oc, xl)
-    gram_part(oc, xr)
-    row_id = lax.broadcasted_iota(jnp.int32, (chunk, chunk), 0)
-    col_id = lax.broadcasted_iota(jnp.int32, (chunk, chunk), 1)
-    wt[z, c, yl, x] = jnp.where(row_id == col_id, jnp.zeros((), BF16), wt[z, c, yl, x])
-    arrive(1)
     sibling(0)
     for cp in slab_fwd:
         cp.wait_recv()
@@ -340,6 +339,9 @@
     r, l = {}, {}
     r[0], l[0] = send_parts(0)
     r[1], l[1] = send_parts(2)
+    for part in (xl, xr):
+        for f in (zr, z2, zl):
+            gram(f, oc, yl, part)
     for q in range(4):
         gram_other(q, (xl, xr))
     a, b = products([(xr, 0), (xl, 2)], blocks)
@@ -362,8 +364,14 @@
     keep(10, a + taken(2))
     keep(11, b + taken(3))
     r[5], l[5] = send_halves(10)
+    gram(zl, c, yl, x)
+    gram(z2, oc, yl, x)
+    gram(zl, oc, yl, x)
     for q in range(4):
         gram_other(q, (x,))
+    row_id = lax.broadcasted_iota(jnp.int32, (chunk, chunk), 0)
+    col_id = lax.broadcasted_iota(jnp.int32, (chunk, chunk), 1)
+    wt[z, c, yl, x] = jnp.where(row_id == col_id, jnp.zeros((), BF16), wt[z, c, yl, x])
 
     for cp in square_copies:
         cp.wait_recv()

time: 79.3 us -> 82.2 us (1.037)
  Pallas kernels: 75.5 us -> 78.5 us
    pallas_call x1, Pallas kernels: 75.5 us -> 78.5 us  [on_device(): pl.pallas_call(kernel, out_shape=[jax.ShapeDtypeStruct((2, rows, cols), B...]
where the time goes in v7:
time: 82.2 us; the launch traced here: 82 us
  Pallas kernels  78.5 us (95%)
  other arithmetic  2.23 us (3%)
    pallas_call x1, Pallas kernels, on_device(): pl.pallas_call(kernel, out_shape=[jax.ShapeDtypeStruct((2, rows, cols), B...  78.5 us
    add x1, other arithmetic, on_device(): dz_b = pull_b * (z_b - mean_b) - difference + cov[1].astype(F32)  2.23 us

profile of v7, /device:TPU:0, one launch (start us, length us, event | category | flops | bytes accessed | tf_op | source)
XLA Modules:
  0.0 82.0 jit_solution(11196378218106572059)
XLA Ops:
  0.6 0.0 copy-start
  0.6 0.0 copy-start.1
  0.6 78.5 %vicreg.1 = (bf16[2,128,1024]{2,1,0:T(8,128)(2,1)}, f32[1,1024]{1,0:T(1,128)}, f32[1,1024]{1,0:T(1,128)}, f32[1,1024]{1,0:T(1,128)}, f32[1,1024]{1,0:T(1,128)}) custom-call(f32[128,1024]{1,0:T(8,128)} %za_hbm.1, f32[128,1024]{1,0:T(8,128)} %zb_hbm.1), custom_call_target="tpu_custom_call" | custom-call | tf_op jit(solution)/shard_map/vicreg/pallas_call | solution.py:428
  79.1 0.0 copy-start.5
  79.1 0.0 copy-start.4
  79.1 0.0 copy-start.3
  79.1 0.0 copy-start.2
  79.2 0.0 copy-done
  79.2 0.0 copy-done.1
  79.2 0.6 copy-done.5
  79.8 0.0 copy-done.4
  79.8 0.0 copy-done.3
  79.8 0.0 copy-done.2
  79.8 2.2 %convert_add_fusion = (f32[128,1024]{1,0:T(8,128)}, f32[128,1024]{1,0:T(8,128)}) fusion(f32[128,1024]{1,0:T(8,128)S(1)} %copy-done, f32[128,1024]{1,0:T(8,128)S(1)} %copy-done.1, bf16[2,128,1024]{2,1,0:T(8,128)(2,1)} %get-tuple-element.9, f32[1024]{0:T(1024)S(1)} %bitcast.11, f32[1024]{0:T(1024)S(1)} %bitcast.13, f32[1024]{0:T(1024)S(1)} %bitcast.10, ...), kind=kLoop, calls=%fused_computation | loop fusion | flops 1572864 | bytes 2637824 | tf_op jit(solution)/shard_map/add | solution.py:456
Async XLA Ops:
  0.6 78.5 %copy-start = (f32[128,1024]{1,0:T(8,128)S(1)}, f32[128,1024]{1,0:T(8,128)}, u32[]{:S(2)}) copy-start(f32[128,1024]{1,0:T(8,128)} %zb_hbm.1) | copy-start | bytes 1572868
  0.6 78.5 %copy-start.1 = (f32[128,1024]{1,0:T(8,128)S(1)}, f32[128,1024]{1,0:T(8,128)}, u32[]{:S(2)}) copy-start(f32[128,1024]{1,0:T(8,128)} %za_hbm.1) | copy-start | bytes 1572868
  79.1 0.7 copy-start.5
  79.1 0.7 copy-start.4
  79.1 0.7 copy-start.3
  79.1 0.7 copy-start.2

commit v8 on v6

--- a/solution.py
+++ b/solution.py
@@ -329,16 +329,19 @@
     def taken(slot):
         return part_in[slot].astype(F32).reshape(pair, chunk)
 
-    turn = [(x2, 2), (x2, 0), (x2, 1), (x2, 3)]
+    turn = [(x2, 2), (x2, 0)]
     for i, acc in enumerate(products(turn, blocks[:14])):
         own[i] = acc
     arrive(3)
     sibling(3)
     gram_other(3, (x2,))
-    for i, acc in enumerate(products(turn, blocks[14:], [own[i] for i in range(4)])):
+    for i, acc in enumerate(products(turn, blocks[14:], [own[i] for i in range(2)])):
         keep(i, acc)
     r, l = {}, {}
     r[0], l[0] = send_parts(0)
+    a, b = products([(x2, 1), (x2, 3)], blocks)
+    keep(2, a)
+    keep(3, b)
     r[1], l[1] = send_parts(2)
     for q in range(4):
         gram_other(q, (xl, xr))

time: 79.3 us -> 78.4 us (0.989)
  Pallas kernels: 75.5 us -> 74.7 us
    pallas_call x1, Pallas kernels: 75.5 us -> 74.7 us  [on_device(): pl.pallas_call(kernel, out_shape=[jax.ShapeDtypeStruct((2, rows, cols), B...]
where the time goes in v8:
time: 78.4 us; the launch traced here: 78.3 us
  Pallas kernels  74.7 us (95%)
  other arithmetic  2.23 us (3%)
    pallas_call x1, Pallas kernels, on_device(): pl.pallas_call(kernel, out_shape=[jax.ShapeDtypeStruct((2, rows, cols), B...  74.7 us
    add x1, other arithmetic, on_device(): dz_b = pull_b * (z_b - mean_b) - difference + cov[1].astype(F32)  2.23 us

profile of v8, /device:TPU:0, one launch (start us, length us, event | category | flops | bytes accessed | tf_op | source)
XLA Modules:
  0.0 78.3 jit_solution(16770524858810987282)
XLA Ops:
  0.6 0.0 copy-start
  0.6 0.0 copy-start.1
  0.6 74.7 %vicreg.1 = (bf16[2,128,1024]{2,1,0:T(8,128)(2,1)}, f32[1,1024]{1,0:T(1,128)}, f32[1,1024]{1,0:T(1,128)}, f32[1,1024]{1,0:T(1,128)}, f32[1,1024]{1,0:T(1,128)}) custom-call(f32[128,1024]{1,0:T(8,128)} %za_hbm.1, f32[128,1024]{1,0:T(8,128)} %zb_hbm.1), custom_call_target="tpu_custom_call" | custom-call | tf_op jit(solution)/shard_map/vicreg/pallas_call | solution.py:423
  75.3 0.0 copy-start.5
  75.3 0.0 copy-start.4
  75.3 0.0 copy-start.3
  75.4 0.0 copy-start.2
  75.4 0.0 copy-done
  75.4 0.0 copy-done.1
  75.4 0.6 copy-done.5
  76.0 0.0 copy-done.4
  76.0 0.0 copy-done.3
  76.0 0.0 copy-done.2
  76.0 2.2 %convert_add_fusion = (f32[128,1024]{1,0:T(8,128)}, f32[128,1024]{1,0:T(8,128)}) fusion(f32[128,1024]{1,0:T(8,128)S(1)} %copy-done, f32[128,1024]{1,0:T(8,128)S(1)} %copy-done.1, bf16[2,128,1024]{2,1,0:T(8,128)(2,1)} %get-tuple-element.9, f32[1024]{0:T(1024)S(1)} %bitcast.11, f32[1024]{0:T(1024)S(1)} %bitcast.13, f32[1024]{0:T(1024)S(1)} %bitcast.10, ...), kind=kLoop, calls=%fused_computation | loop fusion | flops 1572864 | bytes 2637824 | tf_op jit(solution)/shard_map/add | solution.py:451
Async XLA Ops:
  0.6 74.7 %copy-start = (f32[128,1024]{1,0:T(8,128)S(1)}, f32[128,1024]{1,0:T(8,128)}, u32[]{:S(2)}) copy-start(f32[128,1024]{1,0:T(8,128)} %zb_hbm.1) | copy-start | bytes 1572868
  0.6 74.7 %copy-start.1 = (f32[128,1024]{1,0:T(8,128)S(1)}, f32[128,1024]{1,0:T(8,128)}, u32[]{:S(2)}) copy-start(f32[128,1024]{1,0:T(8,128)} %za_hbm.1) | copy-start | bytes 1572868
  75.3 0.7 copy-start.5
  75.3 0.7 copy-start.4
  75.3 0.7 copy-start.3
  75.4 0.7 copy-start.2

commit v9 on v8

--- a/solution.py
+++ b/solution.py
@@ -13,7 +13,7 @@
 MESH = pl.DeviceIdType.MESH
 F32 = jnp.float32
 BF16 = jnp.bfloat16
-N_COPIES = 136
+N_COPIES = 152
 
 
 def kernel(za_hbm, zb_hbm, cov, mean_a, mean_b, pull_a, pull_b, za, zb, sums, squares, zi, stage, jt, wt, part_out, part_in, own, rows_out, rows_in, ls, ss, rs):
@@ -166,14 +166,26 @@
     def to_other(ref):
         return copy(ref, ref, dev(yl_=oyl))
 
+    def share_rows(q, zq):
+        share(("same", q, len([key for key in shared if key[:2] == ("same", q)])), zi.at[plus(z, q), c, yl, zq])
+
+    def same(q):
+        for i in range(4):
+            shared["same", q, i].wait_recv()
+
+    for q in range(4):
+        share_rows(q, z)
+
     ra[0].wait_recv()
     rb[0].wait_recv()
     slab_send(-1)
     near_left = to_other(zi.at[z, c, yl, zl])
+    share_rows(0, zl)
     la[0].wait_recv()
     lb[0].wait_recv()
     slab_send(1)
     near_right = to_other(zi.at[z, c, yl, zr])
+    share_rows(0, zr)
     across = {q: [] for q in range(4)}
 
     def opposite_mine(q):
@@ -183,7 +195,7 @@
     def opposite_others(q):
         fl[q].wait_recv()
         across[q].append(to_other(zi.at[plus(z, q), c, yl, z2, oyh]))
-        share(("same", q), zi.at[plus(z, q), c, yl])
+        share_rows(q, z2)
 
     lb[1].wait_recv()
     fl[0] = forward_left(from_right_f[1])
@@ -202,10 +214,14 @@
         la[s].wait_recv()
     rb[1].wait_recv()
     opposite_mine(1)
+    share_rows(1, zl)
+    share_rows(3, zr)
+    share_rows(1, zr)
     opposite_others(0)
     slab_send(2)
     lb[3].wait_recv()
     fl[3] = forward_left(from_right_f[3])
+    share_rows(2, zr)
     opposite_mine(2)
     opposite_mine(3)
 
@@ -240,9 +256,11 @@
     slab_forward(1)
     rb[2].wait_recv()
     rb[3].wait_recv()
+    share_rows(2, zl)
+    share_rows(3, zl)
     opposite_others(1)
     direct(2)
-    shared["same", 0].wait_recv()
+    same(0)
     gram(z, c, yl, x)
     gram(z, oc, yl, x)
     gram(zr, c, yl, x)
@@ -265,20 +283,13 @@
         for name in ("own", "left", "right", "across"):
             shared[name, q].wait_recv()
 
-    gram(z2, c, yl, x)
-    gram(zl, c, yl, x)
     gram_part(c, xl)
     gram_part(c, xr)
     arrive(0)
     for q in range(1, 4):
-        shared["same", q].wait_recv()
-    for q in range(1, 4):
-        gram(plus(z, q), oc, yl, x)
+        same(q)
     gram_part(oc, xl)
     gram_part(oc, xr)
-    row_id = lax.broadcasted_iota(jnp.int32, (chunk, chunk), 0)
-    col_id = lax.broadcasted_iota(jnp.int32, (chunk, chunk), 1)
-    wt[z, c, yl, x] = jnp.where(row_id == col_id, jnp.zeros((), BF16), wt[z, c, yl, x])
     arrive(1)
     sibling(0)
     for cp in slab_fwd:
@@ -365,8 +376,15 @@
     keep(10, a + taken(2))
     keep(11, b + taken(3))
     r[5], l[5] = send_halves(10)
+    gram(z2, c, yl, x)
+    gram(zl, c, yl, x)
+    for q in range(1, 4):
+        gram(plus(z, q), oc, yl, x)
     for q in range(4):
         gram_other(q, (x,))
+    row_id = lax.broadcasted_iota(jnp.int32, (chunk, chunk), 0)
+    col_id = lax.broadcasted_iota(jnp.int32, (chunk, chunk), 1)
+    wt[z, c, yl, x] = jnp.where(row_id == col_id, jnp.zeros((), BF16), wt[z, c, yl, x])
 
     for cp in square_copies:
         cp.wait_recv()

time: 78.4 us -> 82.7 us (1.055)
  Pallas kernels: 74.7 us -> 78.9 us
    pallas_call x1, Pallas kernels: 74.7 us -> 78.9 us  [on_device(): pl.pallas_call(kernel, out_shape=[jax.ShapeDtypeStruct((2, rows, cols), B...]
where the time goes in v9:
time: 82.7 us; the launch traced here: 82.5 us
  Pallas kernels  78.9 us (95%)
  other arithmetic  2.23 us (3%)
    pallas_call x1, Pallas kernels, on_device(): pl.pallas_call(kernel, out_shape=[jax.ShapeDtypeStruct((2, rows, cols), B...  78.9 us
    add x1, other arithmetic, on_device(): dz_b = pull_b * (z_b - mean_b) - difference + cov[1].astype(F32)  2.23 us

profile of v9, /device:TPU:0, one launch (start us, length us, event | category | flops | bytes accessed | tf_op | source)
XLA Modules:
  0.0 82.5 jit_solution(5601506328196886371)
XLA Ops:
  0.6 0.0 copy-start
  0.6 0.0 copy-start.1
  0.6 78.9 %vicreg.1 = (bf16[2,128,1024]{2,1,0:T(8,128)(2,1)}, f32[1,1024]{1,0:T(1,128)}, f32[1,1024]{1,0:T(1,128)}, f32[1,1024]{1,0:T(1,128)}, f32[1,1024]{1,0:T(1,128)}) custom-call(f32[128,1024]{1,0:T(8,128)} %za_hbm.1, f32[128,1024]{1,0:T(8,128)} %zb_hbm.1), custom_call_target="tpu_custom_call" | custom-call | tf_op jit(solution)/shard_map/vicreg/pallas_call | solution.py:441
  79.6 0.0 copy-start.5
  79.6 0.0 copy-start.4
  79.6 0.0 copy-start.3
  79.6 0.0 copy-start.2
  79.6 0.0 copy-done
  79.6 0.0 copy-done.1
  79.6 0.6 copy-done.5
  80.3 0.0 copy-done.4
  80.3 0.0 copy-done.3
  80.3 0.0 copy-done.2
  80.3 2.2 %convert_add_fusion = (f32[128,1024]{1,0:T(8,128)}, f32[128,1024]{1,0:T(8,128)}) fusion(f32[128,1024]{1,0:T(8,128)S(1)} %copy-done, f32[128,1024]{1,0:T(8,128)S(1)} %copy-done.1, bf16[2,128,1024]{2,1,0:T(8,128)(2,1)} %get-tuple-element.9, f32[1024]{0:T(1024)S(1)} %bitcast.11, f32[1024]{0:T(1024)S(1)} %bitcast.13, f32[1024]{0:T(1024)S(1)} %bitcast.10, ...), kind=kLoop, calls=%fused_computation | loop fusion | flops 1572864 | bytes 2637824 | tf_op jit(solution)/shard_map/add | solution.py:469
Async XLA Ops:
  0.6 79.0 %copy-start = (f32[128,1024]{1,0:T(8,128)S(1)}, f32[128,1024]{1,0:T(8,128)}, u32[]{:S(2)}) copy-start(f32[128,1024]{1,0:T(8,128)} %zb_hbm.1) | copy-start | bytes 1572868
  0.6 79.0 %copy-start.1 = (f32[128,1024]{1,0:T(8,128)S(1)}, f32[128,1024]{1,0:T(8,128)}, u32[]{:S(2)}) copy-start(f32[128,1024]{1,0:T(8,128)} %za_hbm.1) | copy-start | bytes 1572868
  79.6 0.7 copy-start.5
  79.6 0.7 copy-start.4
  79.6 0.7 copy-start.3
  79.6 0.7 copy-start.2

commit v10 on v9

--- a/solution.py
+++ b/solution.py
@@ -283,13 +283,20 @@
         for name in ("own", "left", "right", "across"):
             shared[name, q].wait_recv()
 
+    gram(z2, c, yl, x)
+    gram(zl, c, yl, x)
     gram_part(c, xl)
     gram_part(c, xr)
     arrive(0)
     for q in range(1, 4):
         same(q)
+    for q in range(1, 4):
+        gram(plus(z, q), oc, yl, x)
     gram_part(oc, xl)
     gram_part(oc, xr)
+    row_id = lax.broadcasted_iota(jnp.int32, (chunk, chunk), 0)
+    col_id = lax.broadcasted_iota(jnp.int32, (chunk, chunk), 1)
+    wt[z, c, yl, x] = jnp.where(row_id == col_id, jnp.zeros((), BF16), wt[z, c, yl, x])
     arrive(1)
     sibling(0)
     for cp in slab_fwd:
@@ -376,15 +383,8 @@
     keep(10, a + taken(2))
     keep(11, b + taken(3))
     r[5], l[5] = send_halves(10)
-    gram(z2, c, yl, x)
-    gram(zl, c, yl, x)
-    for q in range(1, 4):
-        gram(plus(z, q), oc, yl, x)
     for q in range(4):
         gram_other(q, (x,))
-    row_id = lax.broadcasted_iota(jnp.int32, (chunk, chunk), 0)
-    col_id = lax.broadcasted_iota(jnp.int32, (chunk, chunk), 1)
-    wt[z, c, yl, x] = jnp.where(row_id == col_id, jnp.zeros((), BF16), wt[z, c, yl, x])
 
     for cp in square_copies:
         cp.wait_recv()

time: 82.7 us -> 78.8 us (0.953)
  Pallas kernels: 78.9 us -> 75 us
    pallas_call x1, Pallas kernels: 78.9 us -> 75 us  [on_device(): pl.pallas_call(kernel, out_shape=[jax.ShapeDtypeStruct((2, rows, cols), B...]
where the time goes in v10:
time: 78.8 us; the launch traced here: 78.6 us
  Pallas kernels  75 us (95%)
  other arithmetic  2.23 us (3%)
    pallas_call x1, Pallas kernels, on_device(): pl.pallas_call(kernel, out_shape=[jax.ShapeDtypeStruct((2, rows, cols), B...  75 us
    add x1, other arithmetic, on_device(): dz_b = pull_b * (z_b - mean_b) - difference + cov[1].astype(F32)  2.23 us

profile of v10, /device:TPU:0, one launch (start us, length us, event | category | flops | bytes accessed | tf_op | source)
XLA Modules:
  0.0 78.6 jit_solution(5424874569577598625)
XLA Ops:
  0.6 0.0 copy-start
  0.6 0.0 copy-start.1
  0.6 75.0 %vicreg.1 = (bf16[2,128,1024]{2,1,0:T(8,128)(2,1)}, f32[1,1024]{1,0:T(1,128)}, f32[1,1024]{1,0:T(1,128)}, f32[1,1024]{1,0:T(1,128)}, f32[1,1024]{1,0:T(1,128)}) custom-call(f32[128,1024]{1,0:T(8,128)} %za_hbm.1, f32[128,1024]{1,0:T(8,128)} %zb_hbm.1), custom_call_target="tpu_custom_call" | custom-call | tf_op jit(solution)/shard_map/vicreg/pallas_call | solution.py:441
  75.6 0.0 copy-start.5
  75.6 0.0 copy-start.4
  75.7 0.0 copy-start.3
  75.7 0.0 copy-start.2
  75.7 0.0 copy-done
  75.7 0.0 copy-done.1
  75.7 0.6 copy-done.5
  76.3 0.0 copy-done.4
  76.3 0.0 copy-done.3
  76.3 0.0 copy-done.2
  76.3 2.2 %convert_add_fusion = (f32[128,1024]{1,0:T(8,128)}, f32[128,1024]{1,0:T(8,128)}) fusion(f32[128,1024]{1,0:T(8,128)S(1)} %copy-done, f32[128,1024]{1,0:T(8,128)S(1)} %copy-done.1, bf16[2,128,1024]{2,1,0:T(8,128)(2,1)} %get-tuple-element.9, f32[1024]{0:T(1024)S(1)} %bitcast.11, f32[1024]{0:T(1024)S(1)} %bitcast.13, f32[1024]{0:T(1024)S(1)} %bitcast.10, ...), kind=kLoop, calls=%fused_computation | loop fusion | flops 1572864 | bytes 2637824 | tf_op jit(solution)/shard_map/add | solution.py:469
Async XLA Ops:
  0.6 75.0 %copy-start = (f32[128,1024]{1,0:T(8,128)S(1)}, f32[128,1024]{1,0:T(8,128)}, u32[]{:S(2)}) copy-start(f32[128,1024]{1,0:T(8,128)} %zb_hbm.1) | copy-start | bytes 1572868
  0.6 75.0 %copy-start.1 = (f32[128,1024]{1,0:T(8,128)S(1)}, f32[128,1024]{1,0:T(8,128)}, u32[]{:S(2)}) copy-start(f32[128,1024]{1,0:T(8,128)} %za_hbm.1) | copy-start | bytes 1572868
  75.6 0.7 copy-start.5
  75.6 0.7 copy-start.4
  75.7 0.7 copy-start.3
  75.7 0.7 copy-start.2

commit v11 on v8

--- a/solution.py
+++ b/solution.py
@@ -16,7 +16,7 @@
 N_COPIES = 136
 
 
-def kernel(za_hbm, zb_hbm, cov, mean_a, mean_b, pull_a, pull_b, za, zb, sums, squares, zi, stage, jt, wt, part_out, part_in, own, rows_out, rows_in, ls, ss, rs):
+def kernel(za_hbm, zb_hbm, cov, mean_a, mean_b, pull_a, pull_b, za, zb, coefs, sums, squares, zi, stage, jt, wt, part_out, part_in, own, rows_out, rows_in, ls, ss, rs):
     dp = lax.axis_index("dp")
     mp = lax.axis_index("mp")
     yh, z = dp // 4, dp % 4
@@ -375,8 +375,18 @@
         variance = variance + squares[d]
     spread = jnp.sqrt(variance / (n_rows - 1) + DEVIATION_FLOOR)
     pull = jnp.where(spread < 1.0, -(VARIANCE_WEIGHT * n_rows / (2.0 * (n_rows - 1))) / spread, 0.0)
-    mean_a[...], mean_b[...] = mean[0:1, :], mean[1:2, :]
-    pull_a[...], pull_b[...] = pull[0:1, :], pull[1:2, :]
+    written = []
+
+    def write(src, dst):
+        cp = pltpu.make_async_copy(src, dst, ls.at[2 + len(written)])
+        cp.start()
+        written.append(cp)
+
+    for i, (value, ref) in enumerate(
+        ((mean[0:1, :], mean_a), (mean[1:2, :], mean_b), (pull[0:1, :], pull_a), (pull[1:2, :], pull_b))
+    ):
+        coefs[i] = value
+        write(coefs.at[i], ref)
 
     for k in (2, 1):
         a, b = products([(x, k), (x, (k + 2) % 4)], blocks)
@@ -392,7 +402,7 @@
         total = own[k, rows, :] + (part_in[straight, p].astype(F32) + part_in[summed, p].astype(F32))
         rows_out[zq, p] = total.astype(BF16)
         if k or not which:
-            back.append(copy(rows_out.at[zq, p], rows_in.at[yh, z], dev(yh_=p, z_=zq)))
+            back.append((copy(rows_out.at[zq, p], rows_in.at[yh, z], dev(yh_=p, z_=zq)), p, plus(z, -k)))
         else:
             rows_in[yh, z] = rows_out[z, yh]
 
@@ -406,11 +416,15 @@
     for which in (0, 1):
         give(1, which, 7, 10, r[5])
         give(3, which, 6, 11, l[5])
-    for cp in back:
+    def write_rows(v, f):
+        write(rows_in.at[v, f], cov.at[v, :, pl.ds(pl.multiple_of(f * chunk, chunk), chunk)])
+
+    write_rows(yh, z)
+    for cp, v, f in back:
         cp.wait_recv()
-    for v in range(2):
-        for f in range(4):
-            cov[v, :, f * chunk : (f + 1) * chunk] = rows_in[v, f]
+        write_rows(v, f)
+    for cp in written:
+        cp.wait()
     for cp in sent:
         cp.wait_send()
 
@@ -418,16 +432,16 @@
 def on_device(z_a, z_b):
     rows, cols = z_a.shape
     chunk = cols // 4
-    vmem = pl.BlockSpec(memory_space=pltpu.VMEM)
     hbm = pl.BlockSpec(memory_space=pl.ANY)
     cov, mean_a, mean_b, pull_a, pull_b = pl.pallas_call(
         kernel,
         out_shape=[jax.ShapeDtypeStruct((2, rows, cols), BF16), *[jax.ShapeDtypeStruct((1, cols), F32)] * 4],
         in_specs=[hbm, hbm],
-        out_specs=[vmem] * 5,
+        out_specs=[hbm] * 5,
         scratch_shapes=[
             pltpu.VMEM((rows, cols), F32),
             pltpu.VMEM((rows, cols), F32),
+            pltpu.VMEM((4, 1, cols), F32),
             pltpu.VMEM((8, 2, cols), F32),
             pltpu.VMEM((8, 2, cols), F32),
             pltpu.VMEM((4, 2, 2, 4, 2, rows, chunk), BF16),
@@ -439,7 +453,7 @@
             pltpu.VMEM((4, 2 * rows, chunk), F32),
             pltpu.VMEM((4, 2, rows, chunk), BF16),
             pltpu.VMEM((2, 4, rows, chunk), BF16),
-            pltpu.SemaphoreType.DMA((2,)),
+            pltpu.SemaphoreType.DMA((14,)),
             pltpu.SemaphoreType.DMA((N_COPIES,)),
             pltpu.SemaphoreType.DMA((N_COPIES,)),
         ],

time: 78.4 us -> 78.4 us (level)
  no operation moved by 1% of the time
where the time goes in v11:
time: 78.4 us; the launch traced here: 78.2 us
  Pallas kernels  74.6 us (95%)
  other arithmetic  2.23 us (3%)
    pallas_call x1, Pallas kernels, on_device(): pl.pallas_call(kernel, out_shape=[jax.ShapeDtypeStruct((2, rows, cols), B...  74.6 us
    add x1, other arithmetic, on_device(): dz_b = pull_b * (z_b - mean_b) - difference + cov[1].astype(F32)  2.23 us

profile of v11, /device:TPU:0, one launch (start us, length us, event | category | flops | bytes accessed | tf_op | source)
XLA Modules:
  0.0 78.2 jit_solution(9342365112620088929)
XLA Ops:
  0.6 0.0 copy-start
  0.6 0.0 copy-start.1
  0.6 74.6 %vicreg.1 = (bf16[2,128,1024]{2,1,0:T(8,128)(2,1)}, f32[1,1024]{1,0:T(1,128)}, f32[1,1024]{1,0:T(1,128)}, f32[1,1024]{1,0:T(1,128)}, f32[1,1024]{1,0:T(1,128)}) custom-call(f32[128,1024]{1,0:T(8,128)} %za_hbm.1, f32[128,1024]{1,0:T(8,128)} %zb_hbm.1), custom_call_target="tpu_custom_call" | custom-call | tf_op jit(solution)/shard_map/vicreg/pallas_call | solution.py:436
  75.3 0.0 copy-start.5
  75.3 0.0 copy-start.4
  75.3 0.0 copy-start.3
  75.3 0.0 copy-start.2
  75.3 0.0 copy-done
  75.3 0.0 copy-done.1
  75.3 0.6 copy-done.5
  76.0 0.0 copy-done.4
  76.0 0.0 copy-done.3
  76.0 0.0 copy-done.2
  76.0 2.2 %convert_add_fusion = (f32[128,1024]{1,0:T(8,128)}, f32[128,1024]{1,0:T(8,128)}) fusion(f32[128,1024]{1,0:T(8,128)S(1)} %copy-done, f32[128,1024]{1,0:T(8,128)S(1)} %copy-done.1, bf16[2,128,1024]{2,1,0:T(8,128)(2,1)} %get-tuple-element.9, f32[1024]{0:T(1024)S(1)} %bitcast.11, f32[1024]{0:T(1024)S(1)} %bitcast.13, f32[1024]{0:T(1024)S(1)} %bitcast.10, ...), kind=kLoop, calls=%fused_computation | loop fusion | flops 1572864 | bytes 2637824 | tf_op jit(solution)/shard_map/add | solution.py:465
Async XLA Ops:
  0.6 74.7 %copy-start = (f32[128,1024]{1,0:T(8,128)S(1)}, f32[128,1024]{1,0:T(8,128)}, u32[]{:S(2)}) copy-start(f32[128,1024]{1,0:T(8,128)} %zb_hbm.1) | copy-start | bytes 1572868
  0.6 74.7 %copy-start.1 = (f32[128,1024]{1,0:T(8,128)S(1)}, f32[128,1024]{1,0:T(8,128)}, u32[]{:S(2)}) copy-start(f32[128,1024]{1,0:T(8,128)} %za_hbm.1) | copy-start | bytes 1572868
  75.3 0.7 copy-start.5
  75.3 0.7 copy-start.4
  75.3 0.7 copy-start.3
  75.3 0.7 copy-start.2

commit v12 on v8

--- a/solution.py
+++ b/solution.py
@@ -274,8 +274,6 @@
         shared["same", q].wait_recv()
     for q in range(1, 4):
         gram(plus(z, q), oc, yl, x)
-    gram_part(oc, xl)
-    gram_part(oc, xr)
     row_id = lax.broadcasted_iota(jnp.int32, (chunk, chunk), 0)
     col_id = lax.broadcasted_iota(jnp.int32, (chunk, chunk), 1)
     wt[z, c, yl, x] = jnp.where(row_id == col_id, jnp.zeros((), BF16), wt[z, c, yl, x])
@@ -343,6 +341,8 @@
     keep(2, a)
     keep(3, b)
     r[1], l[1] = send_parts(2)
+    gram_part(oc, xl)
+    gram_part(oc, xr)
     for q in range(4):
         gram_other(q, (xl, xr))
     a, b = products([(xr, 0), (xl, 2)], blocks)

time: 78.4 us -> 78.7 us (level)
  no operation moved by 1% of the time
where the time goes in v12:
time: 78.7 us; the launch traced here: 78.5 us
  Pallas kernels  74.9 us (95%)
  other arithmetic  2.23 us (3%)
    pallas_call x1, Pallas kernels, on_device(): pl.pallas_call(kernel, out_shape=[jax.ShapeDtypeStruct((2, rows, cols), B...  74.9 us
    add x1, other arithmetic, on_device(): dz_b = pull_b * (z_b - mean_b) - difference + cov[1].astype(F32)  2.23 us

profile of v12, /device:TPU:0, one launch (start us, length us, event | category | flops | bytes accessed | tf_op | source)
XLA Modules:
  0.0 78.5 jit_solution(1823826692060539000)
XLA Ops:
  0.6 0.0 copy-start
  0.6 0.0 copy-start.1
  0.6 74.9 %vicreg.1 = (bf16[2,128,1024]{2,1,0:T(8,128)(2,1)}, f32[1,1024]{1,0:T(1,128)}, f32[1,1024]{1,0:T(1,128)}, f32[1,1024]{1,0:T(1,128)}, f32[1,1024]{1,0:T(1,128)}) custom-call(f32[128,1024]{1,0:T(8,128)} %za_hbm.1, f32[128,1024]{1,0:T(8,128)} %zb_hbm.1), custom_call_target="tpu_custom_call" | custom-call | tf_op jit(solution)/shard_map/vicreg/pallas_call | solution.py:423
  75.6 0.0 copy-start.5
  75.6 0.0 copy-start.4
  75.6 0.0 copy-start.3
  75.6 0.0 copy-start.2
  75.6 0.0 copy-done
  75.7 0.0 copy-done.1
  75.7 0.6 copy-done.5
  76.3 0.0 copy-done.4
  76.3 0.0 copy-done.3
  76.3 0.0 copy-done.2
  76.3 2.2 %convert_add_fusion = (f32[128,1024]{1,0:T(8,128)}, f32[128,1024]{1,0:T(8,128)}) fusion(f32[128,1024]{1,0:T(8,128)S(1)} %copy-done, f32[128,1024]{1,0:T(8,128)S(1)} %copy-done.1, bf16[2,128,1024]{2,1,0:T(8,128)(2,1)} %get-tuple-element.9, f32[1024]{0:T(1024)S(1)} %bitcast.11, f32[1024]{0:T(1024)S(1)} %bitcast.13, f32[1024]{0:T(1024)S(1)} %bitcast.10, ...), kind=kLoop, calls=%fused_computation | loop fusion | flops 1572864 | bytes 2637824 | tf_op jit(solution)/shard_map/add | solution.py:451
Async XLA Ops:
  0.6 75.0 %copy-start = (f32[128,1024]{1,0:T(8,128)S(1)}, f32[128,1024]{1,0:T(8,128)}, u32[]{:S(2)}) copy-start(f32[128,1024]{1,0:T(8,128)} %zb_hbm.1) | copy-start | bytes 1572868
  0.6 75.0 %copy-start.1 = (f32[128,1024]{1,0:T(8,128)S(1)}, f32[128,1024]{1,0:T(8,128)}, u32[]{:S(2)}) copy-start(f32[128,1024]{1,0:T(8,128)} %za_hbm.1) | copy-start | bytes 1572868
  75.6 0.7 copy-start.5
  75.6 0.7 copy-start.4
  75.6 0.7 copy-start.3
  75.6 0.7 copy-start.2

commit v13 on v8

--- a/solution.py
+++ b/solution.py
@@ -242,13 +242,13 @@
     rb[3].wait_recv()
     opposite_others(1)
     direct(2)
+    slab_forward(2)
+    opposite_others(2)
+    direct(3)
     shared["same", 0].wait_recv()
     gram(z, c, yl, x)
     gram(z, oc, yl, x)
     gram(zr, c, yl, x)
-    slab_forward(2)
-    opposite_others(2)
-    direct(3)
     opposite_others(3)
 
     def arrive(q):

time: 78.4 us -> 80 us (1.020); the launches traced: 78.3 us -> 78.9 us
  no operation moved by 1% of the time
where the time goes in v13:
time: 80 us; the launch traced here: 78.9 us
  Pallas kernels  75.3 us (94%)
  other arithmetic  2.23 us (3%)
    pallas_call x1, Pallas kernels, on_device(): pl.pallas_call(kernel, out_shape=[jax.ShapeDtypeStruct((2, rows, cols), B...  75.3 us
    add x1, other arithmetic, on_device(): dz_b = pull_b * (z_b - mean_b) - difference + cov[1].astype(F32)  2.23 us

profile of v13, /device:TPU:0, one launch (start us, length us, event | category | flops | bytes accessed | tf_op | source)
XLA Modules:
  0.0 78.9 jit_solution(17771743027297618591)
XLA Ops:
  0.6 0.0 copy-start
  0.6 0.0 copy-start.1
  0.6 75.3 %vicreg.1 = (bf16[2,128,1024]{2,1,0:T(8,128)(2,1)}, f32[1,1024]{1,0:T(1,128)}, f32[1,1024]{1,0:T(1,128)}, f32[1,1024]{1,0:T(1,128)}, f32[1,1024]{1,0:T(1,128)}) custom-call(f32[128,1024]{1,0:T(8,128)} %za_hbm.1, f32[128,1024]{1,0:T(8,128)} %zb_hbm.1), custom_call_target="tpu_custom_call" | custom-call | tf_op jit(solution)/shard_map/vicreg/pallas_call | solution.py:423
  76.0 0.0 copy-start.5
  76.0 0.0 copy-start.4
  76.0 0.0 copy-start.3
  76.0 0.0 copy-start.2
  76.0 0.0 copy-done
  76.0 0.0 copy-done.1
  76.0 0.6 copy-done.5
  76.7 0.0 copy-done.4
  76.7 0.0 copy-done.3
  76.7 0.0 copy-done.2
  76.7 2.2 %convert_add_fusion = (f32[128,1024]{1,0:T(8,128)}, f32[128,1024]{1,0:T(8,128)}) fusion(f32[128,1024]{1,0:T(8,128)S(1)} %copy-done, f32[128,1024]{1,0:T(8,128)S(1)} %copy-done.1, bf16[2,128,1024]{2,1,0:T(8,128)(2,1)} %get-tuple-element.9, f32[1024]{0:T(1024)S(1)} %bitcast.11, f32[1024]{0:T(1024)S(1)} %bitcast.13, f32[1024]{0:T(1024)S(1)} %bitcast.10, ...), kind=kLoop, calls=%fused_computation | loop fusion | flops 1572864 | bytes 2637824 | tf_op jit(solution)/shard_map/add | solution.py:451
Async XLA Ops:
  0.6 75.4 %copy-start = (f32[128,1024]{1,0:T(8,128)S(1)}, f32[128,1024]{1,0:T(8,128)}, u32[]{:S(2)}) copy-start(f32[128,1024]{1,0:T(8,128)} %zb_hbm.1) | copy-start | bytes 1572868
  0.6 75.4 %copy-start.1 = (f32[128,1024]{1,0:T(8,128)S(1)}, f32[128,1024]{1,0:T(8,128)}, u32[]{:S(2)}) copy-start(f32[128,1024]{1,0:T(8,128)} %za_hbm.1) | copy-start | bytes 1572868
  76.0 0.7 copy-start.5
  76.0 0.7 copy-start.4
  76.0 0.7 copy-start.3
  76.0 0.7 copy-start.2
